TPU v7x, 256 devices: a whole 4x4x8 slice. The times are simulated.
256 devices in a mesh: fsdp: 128 (over x_lo, z, y, core), opt: 2 (over x_hi).
Axes of the slice: x: 4 (x_hi: 2, x_lo: 2; x = x_hi * 2 + x_lo), y: 4, z: 8, core: 2. Of those that a mesh axis runs over, the one named last changes fastest.
Arguments:
- gradient: bfloat16 [16384, 16384], P(('fsdp', 'opt')), may hold values from -200 to 200
- momentum: float32 [128, 2, 2048, 4, 128], P('fsdp', 'opt'), may hold values from -200 to 200
- head_order: int32 [128], replicated, may hold values from 0 to 127, each once
Outputs:
- update: bfloat16 [16384, 16384], P(('fsdp', 'opt'))
- new_momentum: float32 [128, 2, 2048, 4, 128], P('fsdp', 'opt')
Inputs may be any that keep to these rules, and one draw needn't show every extreme that they name: `head_order`: each of 0 to 127 appears once.
All inputs are finite; a program needn't handle non-finite values.
Results may differ from a plain program's by a relative error of at most 0.001.
Values may be sent and summed in bfloat16 or wider, within the bound.
A program may use at most 128 MiB of HBM per device.

v0:
```python
import math

import jax
import jax.numpy as jnp
from jax import lax
from jax.sharding import PartitionSpec as P

D = 16384
HD = 128
BPG = 4
ROW_SPLIT = 8
ITERS = 5


decay_rate = 0.95
first_coeff = 3.4445
second_coeff = -4.775
third_coeff = 2.0315
epsilon = 1e-07
gain_factor = 0.2


def partner(value, axis, apart):
    mask = 2**apart
    pairs = [(source, source ^ mask) for source in range(lax.axis_size(axis))]
    return lax.ppermute(value, axis, pairs)


def batched(left, right):
    return jnp.einsum("jab,jbc->jac", left, right, precision=lax.Precision.HIGHEST)


def local_gram(values):
    return jnp.einsum("rjc,rjd->jcd", values, values, precision=lax.Precision.HIGHEST)


def gram_sum(partial_value):
    summed = partial_value
    for bit_index in range(ROW_SPLIT.bit_length() - 1):
        summed = summed + partner(summed, "fsdp", bit_index)
    return summed


def norm_sum(partial_value):
    summed = partial_value
    for bit_index in range(ROW_SPLIT.bit_length() - 1):
        summed = summed + partner(summed, "fsdp", bit_index)
    return summed


def per_device(gradient, momentum, head_order):
    fsdp_size = lax.axis_size("fsdp")
    opt_size = lax.axis_size("opt")
    groups = fsdp_size // ROW_SPLIT
    blocks = head_order.shape[0]
    head_size = HD
    src_rows = gradient.shape[0]
    inner = src_rows // ROW_SPLIT
    positions = jnp.arange(blocks, dtype=jnp.int32)
    source_of = jnp.sum(
        jnp.where(head_order[:, None] == positions[None, :], positions[:, None], 0), axis=0
    )
    by_block = jnp.take(gradient.reshape(src_rows, blocks, head_size), source_of, axis=1)
    sectioned = by_block.reshape(inner, ROW_SPLIT, opt_size, groups, BPG, head_size)
    sectioned = sectioned.transpose(3, 1, 2, 0, 4, 5).reshape(
        fsdp_size, opt_size, 1, 1, inner, BPG * head_size
    )
    arrived = lax.all_to_all(
        lax.all_to_all(sectioned, "fsdp", split_axis=0, concat_axis=2, tiled=True),
        "opt",
        split_axis=1,
        concat_axis=3,
        tiled=True,
    )
    local_grad = arrived.reshape(-1, BPG, head_size).astype(jnp.float32)
    previous = momentum.reshape(-1, BPG, head_size)
    new_state = decay_rate * previous + local_grad
    nesterov = local_grad + decay_rate * new_state
    sq_norm = norm_sum(jnp.sum(nesterov * nesterov, axis=(0, 2)))
    inv_norm = 1.0 / (jnp.sqrt(sq_norm) + epsilon)
    iterate = nesterov * inv_norm[None, :, None]
    for step in range(ITERS):
        gram_now = gram_sum(local_gram(iterate))
        poly_term = second_coeff * gram_now + third_coeff * batched(gram_now, gram_now)
        iterate = first_coeff * iterate + jnp.einsum(
            "rjc,jcd->rjd", iterate, poly_term, precision=lax.Precision.HIGHEST
        )
    gain_total = gain_factor * math.sqrt(max(D, HD))
    result = (gain_total * iterate).astype(jnp.bfloat16)
    outgoing = result.reshape(1, 1, fsdp_size, opt_size, inner, BPG * head_size)
    returned = lax.all_to_all(
        lax.all_to_all(outgoing, "fsdp", split_axis=2, concat_axis=0, tiled=True),
        "opt",
        split_axis=3,
        concat_axis=1,
        tiled=True,
    )
    returned = returned.reshape(groups, ROW_SPLIT, opt_size, inner, BPG, head_size)
    returned = returned.transpose(3, 1, 2, 0, 4, 5).reshape(src_rows, blocks, head_size)
    placed = jnp.take(returned, head_order, axis=1).reshape(src_rows, blocks * head_size)
    return (placed, new_state.reshape(momentum.shape))


def solution(mesh):
    in_specs = (P(("fsdp", "opt"), None), P("fsdp", "opt", None, None, None), P())
    out_specs = (P(("fsdp", "opt"), None), P("fsdp", "opt", None, None, None))
    return jax.shard_map(
        per_device, mesh=mesh, in_specs=in_specs, out_specs=out_specs, check_vma=False
    )
```

profile of v0, /device:TPU:1, one launch (start us, length us, event | category | flops | bytes accessed | tf_op | source)
XLA Modules:
  0.0 413.7 jit_solution(4878574906774019104)
XLA Ops:
  7.6 68.5 %all_to_all.48 = bf16[128,2,1,1,8,512]{5,4,1,3,2,0:T(8,128)(2,1)S(1)} all-to-all(bf16[128,2,1,1,8,512]{5,4,1,3,2,0:T(8,128)(2,1)S(1)} %bitcast.94), channel_id=1, replica_groups=mesh['fsdp'=128,'opt'=2] {'fsdp'}, dimensions={0} | all-to-all | bytes 4194304 | tf_op jit(solution)/shard_map/all_to_all | solution.py:69
  81.4 5.3 %copy.137 = f32[1,1,2048,4,128]{2,4,3,1,0:T(8,128)} copy(f32[1,1,2048,4,128]{4,3,2,1,0:T(4,128)} %param.6) | data formatting | bytes 8388608 | tf_op args[1]
  86.7 20.5 %all-to-all-done.1 = bf16[1,2,128,1,8,512]{5,4,2,3,0,1:T(8,128)(2,1)S(1)} async-done(((bf16[1,2,128,1,8,512]{5,4,2,3,0,1:T(8,128)(2,1)}), bf16[1,2,128,1,8,512]{5,4,2,3,0,1:T(8,128)(2,1)S(1)}, u32[]{:S(2)}, u32[]{:S(2)}) %all-to-all-start.1) | async-done | bytes 2097184 | tf_op jit(solution)/shard_map/all_to_all | solution.py:68
  113.7 5.3 %copy.162 = f32[1,1,2048,4,128]{2,4,3,1,0:T(8,128)} copy(f32[1,1,2048,4,128]{4,3,1,2,0:T(4,128)} %bitcast.89) | data formatting | bytes 8388608 | tf_op jit(solution)/shard_map/convert_element_type | solution.py:75
  119.0 8.3 %fusion.43 = (f32[1,1,2048,4,128]{2,4,3,1,0:T(8,128)}, f32[1,1,2048,4,128]{2,4,3,1,0:T(8,128)}) fusion(f32[1,1,2048,4,128]{2,4,3,1,0:T(8,128)} %copy.162, f32[1,1,2048,4,128]{2,4,3,1,0:T(8,128)} %copy.137), kind=kLoop, calls=%fused_computation.72 | loop fusion | flops 2097152 | bytes 16777216 | tf_op jit(solution)/shard_map/add | solution.py:77
  127.3 5.2 %copy.140 = f32[1,1,2048,4,128]{4,3,1,2,0:T(4,128)} copy(f32[1,1,2048,4,128]{2,4,3,1,0:T(8,128)} %get-tuple-element.16) | data formatting | bytes 8388608 | tf_op jit(solution)/shard_map/mul | solution.py:77
  132.6 10.1 %fusion.7 = f32[512]{0:T(512)S(1)} fusion(f32[1,1,128,2,1,8,512]{6,1,5,3,2,4,0:T(1,128)} %bitcast.91, f32[1,2,128,1,8,512]{5,4,1,2,3,0:T(8,128)} %copy-done.2), kind=kLoop, calls=%fused_computation.17 | loop fusion | flops 5242368 | bytes 8390656 | tf_op jit(solution)/shard_map/reduce_sum | solution.py:79
  142.9 5.3 %copy.139 = f32[2048,4,128]{0,2,1:T(8,128)} copy(f32[2048,4,128]{2,1,0:T(4,128)} %bitcast.90) | data formatting | bytes 8388608 | tf_op jit(solution)/shard_map/convert_element_type | solution.py:75
  155.1 11.3 %fusion.33 = f32[4,128,128]{2,1,0:T(8,128)S(1)} fusion(f32[2048,4,128]{0,2,1:T(8,128)} %copy.139, f32[4]{0:T(128)S(1)} %add_divide_fusion, f32[1,1,2048,4,128]{2,4,3,1,0:T(8,128)} %copy.137), kind=kOutput, calls=%fused_computation.54 | convolution fusion | flops 1615855616 | bytes 8650768 | tf_op jit(solution)/shard_map/rjc,rjd->jcd/dot_general | solution.py:34
  171.6 6.4 %collective-permute-done.4 = f32[4,128,128]{2,1,0:T(8,128)S(1)} collective-permute-done((f32[4,128,128]{2,1,0:T(8,128)S(1)}, f32[4,128,128]{2,1,0:T(8,128)S(1)}, u32[]{:S(2)}, u32[]{:S(2)}) %collective-permute-start.4) | collective-permute-done | bytes 262176 | tf_op jit(solution)/shard_map/ppermute | solution.py:26
  178.6 7.9 %collective-permute-done.5 = f32[4,128,128]{2,1,0:T(8,128)S(1)} collective-permute-done((f32[4,128,128]{2,1,0:T(8,128)S(1)}, f32[4,128,128]{2,1,0:T(8,128)S(1)}, u32[]{:S(2)}, u32[]{:S(2)}) %collective-permute-start.5) | collective-permute-done | bytes 262176 | tf_op jit(solution)/shard_map/ppermute | solution.py:26
  186.9 5.6 %bitcast_add_fusion.4 = f32[2048,4,128]{0,2,1:T(8,128)S(1)} fusion(f32[4,128,128]{2,1,0:T(8,128)S(1)} %convolution_multiply_fusion.4, f32[4,128,128]{2,1,0:T(8,128)S(1)} %add.117, f32[4,128,128]{2,1,0:T(8,128)S(1)} %collective-permute-done.5, f32[4]{0:T(128)S(1)} %add_divide_fusion, f32[2048,4,128]{0,2,1:T(8,128)S(1)} %copy-done.4, ...), kind=kOutput, calls=%fused_computation.8 | convolution fusion | flops 1623392256 | bytes 13369360 | tf_op jit(solution)/shard_map/rjc,jcd->rjd/dot_general | solution.py:85
  192.4 3.9 fusion.44
  200.9 6.4 %collective-permute-done.7 = f32[4,128,128]{2,1,0:T(8,128)S(1)} collective-permute-done((f32[4,128,128]{2,1,0:T(8,128)S(1)}, f32[4,128,128]{2,1,0:T(8,128)S(1)}, u32[]{:S(2)}, u32[]{:S(2)}) %collective-permute-start.7) | collective-permute-done | bytes 262176 | tf_op jit(solution)/shard_map/ppermute | solution.py:26
  208.0 7.8 %collective-permute-done.8 = f32[4,128,128]{2,1,0:T(8,128)S(1)} collective-permute-done((f32[4,128,128]{2,1,0:T(8,128)S(1)}, f32[4,128,128]{2,1,0:T(8,128)S(1)}, u32[]{:S(2)}, u32[]{:S(2)}) %collective-permute-start.8) | collective-permute-done | bytes 262176 | tf_op jit(solution)/shard_map/ppermute | solution.py:26
  216.2 4.5 %bitcast_add_fusion.3 = f32[2048,4,128]{0,2,1:T(8,128)S(1)} fusion(f32[2048,4,128]{0,2,1:T(8,128)S(1)} %bitcast_add_fusion.4, f32[4,128,128]{2,1,0:T(8,128)S(1)} %convolution_multiply_fusion.3, f32[4,128,128]{2,1,0:T(8,128)S(1)} %add.122, f32[4,128,128]{2,1,0:T(8,128)S(1)} %collective-permute-done.8), kind=kOutput, calls=%fused_computation.7 | convolution fusion | flops 1612906496 | bytes 9175040 | tf_op jit(solution)/shard_map/rjc,jcd->rjd/dot_general | solution.py:85
  220.7 3.9 fusion.45
  229.2 6.4 %collective-permute-done.10 = f32[4,128,128]{2,1,0:T(8,128)S(1)} collective-permute-done((f32[4,128,128]{2,1,0:T(8,128)S(1)}, f32[4,128,128]{2,1,0:T(8,128)S(1)}, u32[]{:S(2)}, u32[]{:S(2)}) %collective-permute-start.10) | collective-permute-done | bytes 262176 | tf_op jit(solution)/shard_map/ppermute | solution.py:26
  236.4 7.8 %collective-permute-done.11 = f32[4,128,128]{2,1,0:T(8,128)S(1)} collective-permute-done((f32[4,128,128]{2,1,0:T(8,128)S(1)}, f32[4,128,128]{2,1,0:T(8,128)S(1)}, u32[]{:S(2)}, u32[]{:S(2)}) %collective-permute-start.11) | collective-permute-done | bytes 262176 | tf_op jit(solution)/shard_map/ppermute | solution.py:26
  244.6 4.4 %bitcast_add_fusion.2 = f32[2048,4,128]{0,2,1:T(8,128)S(1)} fusion(f32[2048,4,128]{0,2,1:T(8,128)S(1)} %bitcast_add_fusion.3, f32[4,128,128]{2,1,0:T(8,128)S(1)} %convolution_multiply_fusion.2, f32[4,128,128]{2,1,0:T(8,128)S(1)} %add.127, f32[4,128,128]{2,1,0:T(8,128)S(1)} %collective-permute-done.11), kind=kOutput, calls=%fused_computation.6 | convolution fusion | flops 1612906496 | bytes 9175040 | tf_op jit(solution)/shard_map/rjc,jcd->rjd/dot_general | solution.py:85
  249.1 3.9 fusion.46
  257.6 6.4 %collective-permute-done.13 = f32[4,128,128]{2,1,0:T(8,128)S(1)} collective-permute-done((f32[4,128,128]{2,1,0:T(8,128)S(1)}, f32[4,128,128]{2,1,0:T(8,128)S(1)}, u32[]{:S(2)}, u32[]{:S(2)}) %collective-permute-start.13) | collective-permute-done | bytes 262176 | tf_op jit(solution)/shard_map/ppermute | solution.py:26
  264.6 7.8 %collective-permute-done.14 = f32[4,128,128]{2,1,0:T(8,128)S(1)} collective-permute-done((f32[4,128,128]{2,1,0:T(8,128)S(1)}, f32[4,128,128]{2,1,0:T(8,128)S(1)}, u32[]{:S(2)}, u32[]{:S(2)}) %collective-permute-start.14) | collective-permute-done | bytes 262176 | tf_op jit(solution)/shard_map/ppermute | solution.py:26
  272.8 4.4 %bitcast_add_fusion.1 = f32[2048,4,128]{0,2,1:T(8,128)S(1)} fusion(f32[2048,4,128]{0,2,1:T(8,128)S(1)} %bitcast_add_fusion.2, f32[4,128,128]{2,1,0:T(8,128)S(1)} %convolution_multiply_fusion.1, f32[4,128,128]{2,1,0:T(8,128)S(1)} %add.132, f32[4,128,128]{2,1,0:T(8,128)S(1)} %collective-permute-done.14), kind=kOutput, calls=%fused_computation.5 | convolution fusion | flops 1612906496 | bytes 9175040 | tf_op jit(solution)/shard_map/rjc,jcd->rjd/dot_general | solution.py:85
  277.3 3.9 fusion.47
  285.8 6.4 %collective-permute-done.16 = f32[4,128,128]{2,1,0:T(8,128)S(1)} collective-permute-done((f32[4,128,128]{2,1,0:T(8,128)S(1)}, f32[4,128,128]{2,1,0:T(8,128)S(1)}, u32[]{:S(2)}, u32[]{:S(2)}) %collective-permute-start.16) | collective-permute-done | bytes 262176 | tf_op jit(solution)/shard_map/ppermute | solution.py:26
  292.8 7.8 %collective-permute-done.17 = f32[4,128,128]{2,1,0:T(8,128)S(1)} collective-permute-done((f32[4,128,128]{2,1,0:T(8,128)S(1)}, f32[4,128,128]{2,1,0:T(8,128)S(1)}, u32[]{:S(2)}, u32[]{:S(2)}) %collective-permute-start.17) | collective-permute-done | bytes 262176 | tf_op jit(solution)/shard_map/ppermute | solution.py:26
  301.0 4.4 %fusion.1 = bf16[2048,4,128]{0,2,1:T(8,128)(2,1)S(1)} fusion(f32[2048,4,128]{0,2,1:T(8,128)S(1)} %bitcast_add_fusion.1, f32[4,128,128]{2,1,0:T(8,128)S(1)} %convolution_multiply_fusion, f32[4,128,128]{2,1,0:T(8,128)S(1)} %add.137, f32[4,128,128]{2,1,0:T(8,128)S(1)} %collective-permute-done.17), kind=kOutput, calls=%fused_computation.4 | convolution fusion | flops 1615003648 | bytes 7077888 | tf_op jit(solution)/shard_map/rjc,jcd->rjd/dot_general | solution.py:85
  310.7 60.6 %all_to_all.49 = bf16[1,1,128,2,8,512]{5,4,3,1,0,2:T(8,128)(2,1)S(1)} all-to-all(bf16[1,1,128,2,8,512]{5,4,3,1,0,2:T(8,128)(2,1)S(1)} %bitcast.96), channel_id=1, replica_groups=mesh['fsdp'=128,'opt'=2] {'fsdp'}, dimensions={2} | all-to-all | bytes 4194304 | tf_op jit(solution)/shard_map/all_to_all | solution.py:92
  376.6 5.2 %copy.163 = f32[1,1,2048,4,128]{4,3,2,1,0:T(4,128)} copy(f32[1,1,2048,4,128]{2,4,3,1,0:T(8,128)} %get-tuple-element.15) | data formatting | bytes 8388608
  381.8 20.3 %all-to-all-done.3 = bf16[128,1,1,2,8,512]{5,4,0,2,1,3:T(8,128)(2,1)S(1)} async-done(((bf16[128,1,1,2,8,512]{5,4,0,2,1,3:T(8,128)(2,1)}), bf16[128,1,1,2,8,512]{5,4,0,2,1,3:T(8,128)(2,1)S(1)}, u32[]{:S(2)}, u32[]{:S(2)}) %all-to-all-start.3) | async-done | bytes 2097184 | tf_op jit(solution)/shard_map/all_to_all | solution.py:91
  406.3 3.9 gather_fusion.1
  (79 shorter events, 71.9 us)
Async XLA Ops:
  0.6 1.6 copy-start
  77.6 29.6 %all-to-all-start.1 = ((bf16[1,2,128,1,8,512]{5,4,2,3,0,1:T(8,128)(2,1)}), bf16[1,2,128,1,8,512]{5,4,2,3,0,1:T(8,128)(2,1)S(1)}, u32[]{:S(2)}, u32[]{:S(2)}) async-start(bf16[1,2,128,1,8,512]{5,4,2,3,0,1:T(8,128)(2,1)} %copy.135), calls=%async_computation.1 | async-start | bytes 4194304 | tf_op jit(solution)/shard_map/all_to_all | solution.py:68
  107.8 2.0 copy-start.2
  142.8 5.4 %collective-permute-start = (f32[4]{0:T(128)S(1)}, f32[4]{0:T(128)S(1)}, u32[]{:S(2)}, u32[]{:S(2)}) collective-permute-start(f32[4]{0:T(128)S(1)} %bitcast_reduce_fusion), channel_id=1, source_target_pairs={{0,2},{2,0},{4,6},{6,4},{8,10},{10,8},{12,14},{14,12},{16,18},{18,... | collective-permute-start | bytes 56 | tf_op jit(solution)/shard_map/ppermute | solution.py:26
  148.2 2.5 collective-permute-start.1
  150.7 4.3 %collective-permute-start.2 = (f32[4]{0:T(128)S(1)}, f32[4]{0:T(128)S(1)}, u32[]{:S(2)}, u32[]{:S(2)}) collective-permute-start(f32[4]{0:T(128)S(1)} %add.113), channel_id=1, source_target_pairs={{0,8},{2,10},{4,12},{6,14},{8,0},{10,2},{12,4},{14,6},{16,24},{18,... | collective-permute-start | bytes 56 | tf_op jit(solution)/shard_map/ppermute | solution.py:26
  155.1 31.8 %copy-start.3 = (f32[1,1,2048,4,128]{2,4,3,1,0:T(8,128)S(1)}, f32[1,1,2048,4,128]{2,4,3,1,0:T(8,128)}, u32[]{:S(2)}) copy-start(f32[1,1,2048,4,128]{2,4,3,1,0:T(8,128)} %copy.137) | copy-start | bytes 12582916
  155.1 31.8 %copy-start.4 = (f32[2048,4,128]{0,2,1:T(8,128)S(1)}, f32[2048,4,128]{0,2,1:T(8,128)}, u32[]{:S(2)}) copy-start(f32[2048,4,128]{0,2,1:T(8,128)} %copy.139) | copy-start | bytes 12582916
  166.4 4.0 collective-permute-start.3
  170.5 7.6 %collective-permute-start.4 = (f32[4,128,128]{2,1,0:T(8,128)S(1)}, f32[4,128,128]{2,1,0:T(8,128)S(1)}, u32[]{:S(2)}, u32[]{:S(2)}) collective-permute-start(f32[4,128,128]{2,1,0:T(8,128)S(1)} %add.116), channel_id=1, source_target_pairs={{0,4},{2,6},{4,0},{6,2},{8,12},{10,14},{12,8},{14,10},{16,20},{18,... | collective-permute-start | bytes 786440 | tf_op jit(solution)/shard_map/ppermute | solution.py:26
  178.1 8.4 %collective-permute-start.5 = (f32[4,128,128]{2,1,0:T(8,128)S(1)}, f32[4,128,128]{2,1,0:T(8,128)S(1)}, u32[]{:S(2)}, u32[]{:S(2)}) collective-permute-start(f32[4,128,128]{2,1,0:T(8,128)S(1)} %add.117), channel_id=1, source_target_pairs={{0,8},{2,10},{4,12},{6,14},{8,0},{10,2},{12,4},{14,6},{16,24},{18,... | collective-permute-start | bytes 786440 | tf_op jit(solution)/shard_map/ppermute | solution.py:26
  196.4 3.4 collective-permute-start.6
  199.8 7.6 %collective-permute-start.7 = (f32[4,128,128]{2,1,0:T(8,128)S(1)}, f32[4,128,128]{2,1,0:T(8,128)S(1)}, u32[]{:S(2)}, u32[]{:S(2)}) collective-permute-start(f32[4,128,128]{2,1,0:T(8,128)S(1)} %add.121), channel_id=1, source_target_pairs={{0,4},{2,6},{4,0},{6,2},{8,12},{10,14},{12,8},{14,10},{16,20},{18,... | collective-permute-start | bytes 786440 | tf_op jit(solution)/shard_map/ppermute | solution.py:26
  207.4 8.4 %collective-permute-start.8 = (f32[4,128,128]{2,1,0:T(8,128)S(1)}, f32[4,128,128]{2,1,0:T(8,128)S(1)}, u32[]{:S(2)}, u32[]{:S(2)}) collective-permute-start(f32[4,128,128]{2,1,0:T(8,128)S(1)} %add.122), channel_id=1, source_target_pairs={{0,8},{2,10},{4,12},{6,14},{8,0},{10,2},{12,4},{14,6},{16,24},{18,... | collective-permute-start | bytes 786440 | tf_op jit(solution)/shard_map/ppermute | solution.py:26
  224.6 3.4 collective-permute-start.9
  228.0 7.6 %collective-permute-start.10 = (f32[4,128,128]{2,1,0:T(8,128)S(1)}, f32[4,128,128]{2,1,0:T(8,128)S(1)}, u32[]{:S(2)}, u32[]{:S(2)}) collective-permute-start(f32[4,128,128]{2,1,0:T(8,128)S(1)} %add.126), channel_id=1, source_target_pairs={{0,4},{2,6},{4,0},{6,2},{8,12},{10,14},{12,8},{14,10},{16,20},{18,... | collective-permute-start | bytes 786440 | tf_op jit(solution)/shard_map/ppermute | solution.py:26
  235.7 8.6 %collective-permute-start.11 = (f32[4,128,128]{2,1,0:T(8,128)S(1)}, f32[4,128,128]{2,1,0:T(8,128)S(1)}, u32[]{:S(2)}, u32[]{:S(2)}) collective-permute-start(f32[4,128,128]{2,1,0:T(8,128)S(1)} %add.127), channel_id=1, source_target_pairs={{0,8},{2,10},{4,12},{6,14},{8,0},{10,2},{12,4},{14,6},{16,24},{18,... | collective-permute-start | bytes 786440 | tf_op jit(solution)/shard_map/ppermute | solution.py:26
  253.0 3.4 collective-permute-start.12
  256.4 7.6 %collective-permute-start.13 = (f32[4,128,128]{2,1,0:T(8,128)S(1)}, f32[4,128,128]{2,1,0:T(8,128)S(1)}, u32[]{:S(2)}, u32[]{:S(2)}) collective-permute-start(f32[4,128,128]{2,1,0:T(8,128)S(1)} %add.131), channel_id=1, source_target_pairs={{0,4},{2,6},{4,0},{6,2},{8,12},{10,14},{12,8},{14,10},{16,20},{18,... | collective-permute-start | bytes 786440 | tf_op jit(solution)/shard_map/ppermute | solution.py:26
  264.1 8.4 %collective-permute-start.14 = (f32[4,128,128]{2,1,0:T(8,128)S(1)}, f32[4,128,128]{2,1,0:T(8,128)S(1)}, u32[]{:S(2)}, u32[]{:S(2)}) collective-permute-start(f32[4,128,128]{2,1,0:T(8,128)S(1)} %add.132), channel_id=1, source_target_pairs={{0,8},{2,10},{4,12},{6,14},{8,0},{10,2},{12,4},{14,6},{16,24},{18,... | collective-permute-start | bytes 786440 | tf_op jit(solution)/shard_map/ppermute | solution.py:26
  281.2 3.4 collective-permute-start.15
  284.6 7.6 %collective-permute-start.16 = (f32[4,128,128]{2,1,0:T(8,128)S(1)}, f32[4,128,128]{2,1,0:T(8,128)S(1)}, u32[]{:S(2)}, u32[]{:S(2)}) collective-permute-start(f32[4,128,128]{2,1,0:T(8,128)S(1)} %add.136), channel_id=1, source_target_pairs={{0,4},{2,6},{4,0},{6,2},{8,12},{10,14},{12,8},{14,10},{16,20},{18,... | collective-permute-start | bytes 786440 | tf_op jit(solution)/shard_map/ppermute | solution.py:26
  292.2 8.4 %collective-permute-start.17 = (f32[4,128,128]{2,1,0:T(8,128)S(1)}, f32[4,128,128]{2,1,0:T(8,128)S(1)}, u32[]{:S(2)}, u32[]{:S(2)}) collective-permute-start(f32[4,128,128]{2,1,0:T(8,128)S(1)} %add.137), channel_id=1, source_target_pairs={{0,8},{2,10},{4,12},{6,14},{8,0},{10,2},{12,4},{14,6},{16,24},{18,... | collective-permute-start | bytes 786440 | tf_op jit(solution)/shard_map/ppermute | solution.py:26
  371.3 5.3 %copy-start.5 = (s32[128]{0:T(128)S(1)}, s32[128]{0:T(128)}, u32[]{:S(2)}) copy-start(s32[128]{0:T(128)} %param.7) | copy-start | bytes 1540
  372.8 29.4 %all-to-all-start.3 = ((bf16[128,1,1,2,8,512]{5,4,0,2,1,3:T(8,128)(2,1)}), bf16[128,1,1,2,8,512]{5,4,0,2,1,3:T(8,128)(2,1)S(1)}, u32[]{:S(2)}, u32[]{:S(2)}) async-start(bf16[128,1,1,2,8,512]{5,4,0,2,1,3:T(8,128)(2,1)} %copy.158), calls=%async_computation.3 | async-start | bytes 4194304 | tf_op jit(solution)/shard_map/all_to_all | solution.py:91
  406.3 7.2 %copy-start.1 = (bf16[64,16384]{1,0:T(8,128)(2,1)S(1)}, bf16[64,16384]{1,0:T(8,128)(2,1)}, u32[]{:S(2)}) copy-start(bf16[64,16384]{1,0:T(8,128)(2,1)} %param.5) | copy-start | bytes 6291460
where the time goes:
time: 421 us; the launch traced here: 414 us
  blocking collectives  129 us (31%)
  waiting for transfers between devices  123 us (29%)
  local copies, waits for them, and re-layouts  54.3 us (13%)
  matrix products  52.2 us (12%)
  starting transfers between devices  29.9 us (7%)
  other arithmetic  24 us (6%)
    ppermute x18, waiting for transfers between devices, partner(): return lax.ppermute(value, axis, pairs)  82.2 us
    all_to_all x1, blocking collectives, per_device(): lax.all_to_all(sectioned, 'fsdp', split_axis=0, concat_axis=2, tiled=True)  68.5 us
    all_to_all x1, blocking collectives, per_device(): lax.all_to_all(outgoing, 'fsdp', split_axis=2, concat_axis=0, tiled=True)  60.6 us
    dot_general x5, matrix products, local_gram(): jnp.einsum('rjc,rjd->jcd', values, values, precision=lax.Precision.HIGHEST)  27 us
    dot_general x5, matrix products, per_device(): jnp.einsum('rjc,jcd->rjd', iterate, poly_term, precision=lax.Precision.HI...  23.3 us
    ppermute x18, starting transfers between devices, partner(): return lax.ppermute(value, axis, pairs)  22.4 us
    all_to_all x1, waiting for transfers between devices, per_device(): lax.all_to_all(lax.all_to_all(sectioned, 'fsdp', split_axis=0, concat_axi...  20.5 us
    all_to_all x1, waiting for transfers between devices, per_device(): lax.all_to_all(lax.all_to_all(outgoing, 'fsdp', split_axis=2, concat_axis...  20.3 us
  transfers between devices with their start and end apart: 20, of which 19 were waited for; matrix products, arithmetic and copies ran while one was open for 4% of the time, Pallas kernels for 0%

commit v1 on v0

--- a/solution.py
+++ b/solution.py
@@ -41,13 +41,6 @@
     return summed
 
 
-def norm_sum(partial_value):
-    summed = partial_value
-    for bit_index in range(ROW_SPLIT.bit_length() - 1):
-        summed = summed + partner(summed, "fsdp", bit_index)
-    return summed
-
-
 def per_device(gradient, momentum, head_order):
     fsdp_size = lax.axis_size("fsdp")
     opt_size = lax.axis_size("opt")
@@ -63,38 +56,30 @@
     by_block = jnp.take(gradient.reshape(src_rows, blocks, head_size), source_of, axis=1)
     sectioned = by_block.reshape(inner, ROW_SPLIT, opt_size, groups, BPG, head_size)
     sectioned = sectioned.transpose(3, 1, 2, 0, 4, 5).reshape(
-        fsdp_size, opt_size, 1, 1, inner, BPG * head_size
+        fsdp_size * opt_size, inner, BPG * head_size
     )
-    arrived = lax.all_to_all(
-        lax.all_to_all(sectioned, "fsdp", split_axis=0, concat_axis=2, tiled=True),
-        "opt",
-        split_axis=1,
-        concat_axis=3,
-        tiled=True,
-    )
+    arrived = lax.all_to_all(sectioned, ("fsdp", "opt"), split_axis=0, concat_axis=0, tiled=True)
     local_grad = arrived.reshape(-1, BPG, head_size).astype(jnp.float32)
     previous = momentum.reshape(-1, BPG, head_size)
     new_state = decay_rate * previous + local_grad
     nesterov = local_grad + decay_rate * new_state
-    sq_norm = norm_sum(jnp.sum(nesterov * nesterov, axis=(0, 2)))
-    inv_norm = 1.0 / (jnp.sqrt(sq_norm) + epsilon)
-    iterate = nesterov * inv_norm[None, :, None]
+    gram_now = gram_sum(local_gram(nesterov))
+    sq_norm = jnp.trace(gram_now, axis1=1, axis2=2)
+    inv_norm = (1.0 / (jnp.sqrt(sq_norm) + epsilon))[:, None, None]
+    gram_now = gram_now * inv_norm * inv_norm
+    gain_total = gain_factor * math.sqrt(max(D, HD))
+    eye = jnp.eye(head_size, dtype=jnp.float32)
+    chain = None
     for step in range(ITERS):
-        gram_now = gram_sum(local_gram(iterate))
-        poly_term = second_coeff * gram_now + third_coeff * batched(gram_now, gram_now)
-        iterate = first_coeff * iterate + jnp.einsum(
-            "rjc,jcd->rjd", iterate, poly_term, precision=lax.Precision.HIGHEST
-        )
-    gain_total = gain_factor * math.sqrt(max(D, HD))
-    result = (gain_total * iterate).astype(jnp.bfloat16)
-    outgoing = result.reshape(1, 1, fsdp_size, opt_size, inner, BPG * head_size)
-    returned = lax.all_to_all(
-        lax.all_to_all(outgoing, "fsdp", split_axis=2, concat_axis=0, tiled=True),
-        "opt",
-        split_axis=3,
-        concat_axis=1,
-        tiled=True,
-    )
+        factor = first_coeff * eye + second_coeff * gram_now + third_coeff * batched(gram_now, gram_now)
+        chain = factor if chain is None else batched(chain, factor)
+        if step < ITERS - 1:
+            gram_now = batched(factor, batched(gram_now, factor))
+    chain = chain * (gain_total * inv_norm)
+    result = jnp.einsum("rjc,jcd->rjd", nesterov, chain, precision=lax.Precision.HIGHEST)
+    result = result.astype(jnp.bfloat16)
+    outgoing = result.reshape(fsdp_size * opt_size, inner, BPG * head_size)
+    returned = lax.all_to_all(outgoing, ("fsdp", "opt"), split_axis=0, concat_axis=0, tiled=True)
     returned = returned.reshape(groups, ROW_SPLIT, opt_size, inner, BPG, head_size)
     returned = returned.transpose(3, 1, 2, 0, 4, 5).reshape(src_rows, blocks, head_size)
     placed = jnp.take(returned, head_order, axis=1).reshape(src_rows, blocks * head_size)

time: 421 us -> 208 us (0.49); the launches traced: 414 us -> 207 us
  waiting for transfers between devices: 123 us -> 56.4 us
  blocking collectives: 129 us -> 68.6 us
  matrix products: 52.2 us -> 18.6 us
  local copies, waits for them, and re-layouts: 54.3 us -> 33.8 us
  starting transfers between devices: 29.9 us -> 12.6 us
  other arithmetic: 24 us -> 16.3 us
    ppermute x18 -> x3, waiting for transfers between devices: 82.2 us -> 14.5 us  [partner(): return lax.ppermute(value, axis, pairs)]
    all_to_all x2 -> x1, blocking collectives: 129 us -> 68.6 us  [per_device(): lax.all_to_all(sectioned, ('fsdp', 'opt'), split_axis=0, concat_axis=0, t...]
    dot_general x5 -> x1, matrix products: 27 us -> 6.81 us  [local_gram(): jnp.einsum('rjc,rjd->jcd', values, values, precision=lax.Precision.HIGHEST)]
    ppermute x18 -> x3, starting transfers between devices: 22.4 us -> 3.55 us  [partner(): return lax.ppermute(value, axis, pairs)]
    dot_general x5 -> x1, matrix products: 23.3 us -> 4.96 us  [per_device(): jnp.einsum('rjc,jcd->rjd', nesterov, chain, precision=lax.Precision.HIGHEST)]
    unnamed x14 -> x4, local copies, waits for them, and re-layouts: 13.2 us -> 0.67 us
    reduce_sum x2 -> x1, other arithmetic: 10.2 us -> 0.13 us  [per_device(): sq_norm = jnp.trace(gram_now, axis1=1, axis2=2)]
    reshape x1 -> x3, local copies, waits for them, and re-layouts: 2.75 us -> 10 us  [the longest x1 5.34 us: per_device(): returned.reshape(groups, ROW_SPLIT, opt_size, inner, BPG, head_size)]
  transfers between devices with their start and end apart: 20 -> 4, of which waited for: 19 -> 4; matrix products, arithmetic and copies ran while one was open for 4% -> 5% of each run, Pallas kernels for 0% -> 0%
where the time goes in v1:
time: 208 us; the launch traced here: 207 us
  blocking collectives  68.6 us (33%)
  waiting for transfers between devices  56.4 us (27%)
  local copies, waits for them, and re-layouts  33.8 us (16%)
  matrix products  18.6 us (9%)
  other arithmetic  16.3 us (8%)
  starting transfers between devices  12.6 us (6%)
    all_to_all x1, blocking collectives, per_device(): lax.all_to_all(sectioned, ('fsdp', 'opt'), split_axis=0, concat_axis=0, t...  68.6 us
    all_to_all x1, waiting for transfers between devices, per_device(): lax.all_to_all(outgoing, ('fsdp', 'opt'), split_axis=0, concat_axis=0, ti...  41.9 us
    ppermute x3, waiting for transfers between devices, partner(): return lax.ppermute(value, axis, pairs)  14.5 us
    convert_element_type x2, local copies, waits for them, and re-layouts, per_device(): local_grad = arrived.reshape(-1, BPG, head_size).astype(jnp.float32)  9.43 us
    all_to_all x1, starting transfers between devices, per_device(): lax.all_to_all(outgoing, ('fsdp', 'opt'), split_axis=0, concat_axis=0, ti...  9.06 us
    dot_general x1, matrix products, local_gram(): jnp.einsum('rjc,rjd->jcd', values, values, precision=lax.Precision.HIGHEST)  6.81 us
    dot_general x17, matrix products, batched(): jnp.einsum('jab,jbc->jac', left, right, precision=lax.Precision.HIGHEST)  6.79 us
    add x1, other arithmetic, per_device(): new_state = decay_rate * previous + local_grad  5.51 us
  transfers between devices with their start and end apart: 4, of which 4 were waited for; matrix products, arithmetic and copies ran while one was open for 5% of the time, Pallas kernels for 0%

profile of v1, /device:TPU:1, one launch (start us, length us, event | category | flops | bytes accessed | tf_op | source)
XLA Modules:
  0.0 207.0 jit_solution(17325406253816576457)
XLA Ops:
  0.6 0.9 select_reduce_fusion.1
  1.6 0.7 copy-done
  2.2 1.9 copy_bitcast_fusion.1
  4.2 3.7 %gather_fusion = bf16[128,64,128]{2,1,0:T(8,128)(2,1)} fusion(bf16[64,128,128]{2,0,1:T(8,128)(2,1)} %copy_bitcast_fusion.1, s32[1024]{0:T(1024)S(1)} %pad_clamp_fusion.1), kind=kCustom, calls=%fused_computation.clone | custom fusion | bytes 4194816 | tf_op jit(solution)/shard_map/jit(_take)/gather | solution.py:56
  7.9 1.9 broadcast_select_fusion
  9.7 0.6 copy.24
  10.4 68.6 %all_to_all.10 = bf16[256,8,512]{2,1,0:T(8,128)(2,1)} all-to-all(bf16[256,8,512]{2,1,0:T(8,128)(2,1)S(1)} %bitcast.63), channel_id=1, replica_groups=mesh['fsdp'=128,'opt'=2] {'fsdp','opt'}, dimensions={0} | all-to-all | bytes 4194304 | tf_op jit(solution)/shard_map/all_to_all | solution.py:61
  79.0 4.7 %reshape.74 = f32[2048,4,128]{2,1,0:T(4,128)} reshape(bf16[256,8,512]{2,1,0:T(8,128)(2,1)} %all_to_all.10) | data formatting | bytes 6291456 | tf_op jit(solution)/shard_map/convert_element_type | solution.py:62
  83.7 4.4 %fusion.1 = f32[2048,4,128]{2,1,0:T(4,128)S(1)} fusion(f32[2048,4,128]{2,1,0:T(4,128)} %reshape.74, f32[1,1,2048,4,128]{4,3,2,1,0:T(4,128)} %param.6), kind=kLoop, calls=%fused_computation.4 | loop fusion | flops 4194304 | bytes 12582912 | tf_op jit(solution)/shard_map/add | solution.py:65
  88.1 6.8 %fusion.4 = f32[4,128,128]{2,1,0:T(8,128)S(1)} fusion(f32[2048,4,128]{2,1,0:T(4,128)S(1)} %fusion.1), kind=kOutput, calls=%fused_computation.7 | convolution fusion | flops 1610612736 | bytes 4456448 | tf_op jit(solution)/shard_map/rjc,rjd->jcd/dot_general | solution.py:34
  95.0 1.5 collective-permute-done
  96.5 0.7 collective-permute-start.1
  97.3 7.3 %collective-permute-done.1 = f32[4,128,128]{2,1,0:T(8,128)S(1)} collective-permute-done((f32[4,128,128]{2,1,0:T(8,128)S(1)}, f32[4,128,128]{2,1,0:T(8,128)S(1)}, u32[]{:S(2)}, u32[]{:S(2)}) %collective-permute-start.1) | collective-permute-done | bytes 262176 | tf_op jit(solution)/shard_map/ppermute | solution.py:26
  104.6 2.7 %collective-permute-start.2 = (f32[4,128,128]{2,1,0:T(8,128)S(1)}, f32[4,128,128]{2,1,0:T(8,128)S(1)}, u32[]{:S(2)}, u32[]{:S(2)}) collective-permute-start(f32[4,128,128]{2,1,0:T(8,128)S(1)} %add.93), channel_id=1, source_target_pairs={{0,8},{2,10},{4,12},{6,14},{8,0},{10,2},{12,4},{14,6},{16,24},{18,... | collective-permute-start | bytes 786440 | tf_op jit(solution)/shard_map/ppermute | solution.py:26
  107.3 5.7 %collective-permute-done.2 = f32[4,128,128]{2,1,0:T(8,128)S(1)} collective-permute-done((f32[4,128,128]{2,1,0:T(8,128)S(1)}, f32[4,128,128]{2,1,0:T(8,128)S(1)}, u32[]{:S(2)}, u32[]{:S(2)}) %collective-permute-start.2) | collective-permute-done | bytes 262176 | tf_op jit(solution)/shard_map/ppermute | solution.py:26
  113.2 0.5 add_add_fusion
  113.7 0.4 fusion.16
  115.4 0.4 fusion.20
  115.8 0.4 fusion.22
  116.5 0.4 fusion.24
  116.9 0.4 fusion.25
  119.7 0.4 convolution_multiply_fusion
  120.1 5.0 %fusion.9 = bf16[2048,4,128]{0,2,1:T(8,128)(2,1)} fusion(f32[4,128,128]{2,1,0:T(8,128)S(1)} %convolution_multiply_fusion, f32[2048,4,128]{2,1,0:T(4,128)S(1)} %fusion.1), kind=kOutput, calls=%fused_computation.11 | convolution fusion | flops 1611661312 | bytes 6553600 | tf_op jit(solution)/shard_map/rjc,jcd->rjd/dot_general | solution.py:79
  125.1 4.2 %copy.29 = bf16[2048,4,128]{2,1,0:T(4,128)(2,1)} copy(bf16[2048,4,128]{0,2,1:T(8,128)(2,1)} %fusion.9) | data formatting | bytes 4194304 | tf_op jit(solution)/shard_map/convert_element_type | solution.py:80
  129.3 4.1 %reshape.70 = bf16[256,8,512]{2,1,0:T(8,128)(2,1)} reshape(bf16[2048,4,128]{2,1,0:T(4,128)(2,1)} %copy.29) | data formatting | bytes 4194304 | tf_op jit(solution)/shard_map/reshape | solution.py:81
  133.4 9.1 %all-to-all-start.1 = ((bf16[256,8,512]{2,1,0:T(8,128)(2,1)}), bf16[256,8,512]{2,1,0:T(8,128)(2,1)}, u32[]{:S(2)}, u32[]{:S(2)}) async-start(bf16[256,8,512]{2,1,0:T(8,128)(2,1)} %reshape.70), calls=%async_computation.1 | async-start | bytes 4194304 | tf_op jit(solution)/shard_map/all_to_all | solution.py:82
  142.6 4.7 %reshape.75 = f32[1,1,2048,4,128]{4,3,2,1,0:T(4,128)} reshape(bf16[256,8,512]{2,1,0:T(8,128)(2,1)} %all_to_all.10) | data formatting | bytes 6291456 | tf_op jit(solution)/shard_map/convert_element_type | solution.py:62
  147.3 5.5 %multiply_add_fusion = f32[1,1,2048,4,128]{4,3,2,1,0:T(4,128)} fusion(f32[1,1,2048,4,128]{4,3,2,1,0:T(4,128)} %reshape.75, f32[1,1,2048,4,128]{4,3,2,1,0:T(4,128)} %param.6), kind=kLoop, calls=%fused_computation.9 | loop fusion | flops 2097152 | bytes 12582912 | tf_op jit(solution)/shard_map/add | solution.py:64
  152.8 41.9 %all-to-all-done.1 = bf16[256,8,512]{2,1,0:T(8,128)(2,1)} async-done(((bf16[256,8,512]{2,1,0:T(8,128)(2,1)}), bf16[256,8,512]{2,1,0:T(8,128)(2,1)}, u32[]{:S(2)}, u32[]{:S(2)}) %all-to-all-start.1) | async-done | bytes 2097184 | tf_op jit(solution)/shard_map/all_to_all | solution.py:82
  194.6 5.3 %copy.30 = bf16[16,8,2,8,4,128]{5,1,3,4,0,2:T(8,128)(2,1)} copy(bf16[16,8,2,8,4,128]{5,3,4,2,1,0:T(8,128)(2,1)} %bitcast.6) | data formatting | bytes 4194304 | tf_op jit(solution)/shard_map/reshape | solution.py:83
  200.0 3.7 %gather_fusion.1 = bf16[128,64,128]{2,1,0:T(8,128)(2,1)} fusion(bf16[64,128,128]{2,0,1:T(8,128)(2,1)} %bitcast.62, s32[1024]{0:T(1024)S(1)} %pad_clamp_fusion), kind=kCustom, calls=%fused_computation.1.clone | custom fusion | bytes 4194816 | tf_op jit(solution)/shard_map/jit(_take)/gather | solution.py:85
  203.7 3.3 %copy_bitcast_fusion = bf16[64,16384]{1,0:T(8,128)(2,1)} fusion(bf16[128,64,128]{2,1,0:T(8,128)(2,1)} %gather_fusion.1, pred[128]{0:T(512)(128)(4,1)S(1)} %compare_and_fusion), kind=kLoop, calls=%fused_computation.12 | loop fusion | flops 1048576 | bytes 4194432 | tf_op jit(solution)/shard_map/reshape | solution.py:85
  (26 shorter events, 4.3 us)
Async XLA Ops:
  0.6 1.6 copy-start
  94.9 1.6 collective-permute-start
  96.5 8.0 %collective-permute-start.1 = (f32[4,128,128]{2,1,0:T(8,128)S(1)}, f32[4,128,128]{2,1,0:T(8,128)S(1)}, u32[]{:S(2)}, u32[]{:S(2)}) collective-permute-start(f32[4,128,128]{2,1,0:T(8,128)S(1)} %add.92), channel_id=1, source_target_pairs={{0,4},{2,6},{4,0},{6,2},{8,12},{10,14},{12,8},{14,10},{16,20},{18,... | collective-permute-start | bytes 786440 | tf_op jit(solution)/shard_map/ppermute | solution.py:26
  104.6 8.4 %collective-permute-start.2 = (f32[4,128,128]{2,1,0:T(8,128)S(1)}, f32[4,128,128]{2,1,0:T(8,128)S(1)}, u32[]{:S(2)}, u32[]{:S(2)}) collective-permute-start(f32[4,128,128]{2,1,0:T(8,128)S(1)} %add.93), channel_id=1, source_target_pairs={{0,8},{2,10},{4,12},{6,14},{8,0},{10,2},{12,4},{14,6},{16,24},{18,... | collective-permute-start | bytes 786440 | tf_op jit(solution)/shard_map/ppermute | solution.py:26
  133.4 9.1 %copy-start.1 = (s32[128]{0:T(128)S(1)}, s32[128]{0:T(128)}, u32[]{:S(2)}) copy-start(s32[128]{0:T(128)} %param.7) | copy-start | bytes 1540
  133.4 61.2 %all-to-all-start.1 = ((bf16[256,8,512]{2,1,0:T(8,128)(2,1)}), bf16[256,8,512]{2,1,0:T(8,128)(2,1)}, u32[]{:S(2)}, u32[]{:S(2)}) async-start(bf16[256,8,512]{2,1,0:T(8,128)(2,1)} %reshape.70), calls=%async_computation.1 | async-start | bytes 4194304 | tf_op jit(solution)/shard_map/all_to_all | solution.py:82

commit v2 on v1

v2 whole, which is shorter than its diff:
```python
import math

import jax
import jax.numpy as jnp
from jax import lax
from jax.experimental import pallas as pl
from jax.experimental.pallas import tpu as pltpu
from jax.sharding import PartitionSpec as P

D = 16384
HD = 128
BPG = 4
ROW_SPLIT = 8
ITERS = 5
NX, NY, NZ, NCORE = 4, 4, 8, 2
NDEV = NX * NY * NZ * NCORE
SUB = 8
CHUNK = SUB * BPG
BATCH = NX * ROW_SPLIT
ROWS = NDEV * CHUNK

decay_rate = 0.95
first_coeff = 3.4445
second_coeff = -4.775
third_coeff = 2.0315
epsilon = 1e-07
gain_factor = 0.2

MESH = pl.DeviceIdType.MESH
HIGHEST = lax.Precision.HIGHEST


def dot(left, right, left_dim=1):
    return lax.dot_general(
        left, right, (((left_dim,), (0,)), ((), ())), precision=HIGHEST, preferred_element_type=jnp.float32
    )


def z_offset(turn):
    back = NZ - 1 - turn
    odd = back % 2
    return odd * ((back + 1) // 2) + (1 - odd) * ((NZ - back // 2) % NZ)


def place(z, x, k):
    return (z * NX + x) * ROW_SPLIT + k, ((x % 2) * NZ + z) * ROW_SPLIT + k, x // 2


def chunk_of(index):
    return pl.ds(pl.multiple_of(index * CHUNK, CHUNK), CHUNK)


def kernel(
    source_ref,
    grad_ref,
    mom_hbm,
    ret_hbm,
    new_hbm,
    mom,
    send,
    recv,
    nest,
    back,
    stage,
    gram,
    gram_in,
    chain,
    send_sem,
    recv_sem,
    back_send_sem,
    back_recv_sem,
    gram_sems,
    chain_sems,
    local_sems,
):
    f, o = lax.axis_index("fsdp"), lax.axis_index("opt")
    my_k = f % ROW_SPLIT
    my_z = (f // ROW_SPLIT) % NZ
    my_x = o * 2 + f // (ROW_SPLIT * NZ)
    my_y, my_core = my_k // 2, my_k % 2
    my_e, _, _ = place(my_z, my_x, my_k)

    mom_in = pltpu.make_async_copy(mom_hbm, mom, local_sems.at[0])
    mom_in.start()

    def target_k(kk):
        return ((my_y + kk // 2) % NY) * 2 + (my_core + kk % 2) % 2

    def send_group(turn, r, own):
        z, x = (my_z + z_offset(turn)) % NZ, (my_x + r) % NX
        group = (x // 2) * 16 + (x % 2) * NZ + z
        for j in range(BPG):
            column = source_ref[group * BPG + j] * HD
            stage[j] = grad_ref[:, pl.ds(column, HD)].astype(jnp.float32)
        for kk in range(ROW_SPLIT):
            k = target_k(kk)
            e, to_f, to_o = place(z, x, k)
            parts = [stage[j, pl.ds(k, SUB, stride=ROW_SPLIT), :] for j in range(BPG)]
            chunk = jnp.concatenate(parts, axis=0).astype(jnp.bfloat16)
            if own and kk == 0:
                recv[chunk_of(my_e), :] = chunk
                continue
            send[chunk_of(e), :] = chunk
            pltpu.make_async_remote_copy(
                src_ref=send.at[chunk_of(e), :],
                dst_ref=recv.at[chunk_of(my_e), :],
                send_sem=send_sem,
                recv_sem=recv_sem.at[turn],
                device_id=(to_f, to_o),
                device_id_type=MESH,
            ).start()

    def send_turn(index, carry):
        send_group(index // NX, index % NX, False)
        return carry

    lax.fori_loop(0, (NZ - 1) * NX, send_turn, 0)
    send_group(NZ - 1, 0, True)

    def send_last(r, carry):
        send_group(NZ - 1, r, False)
        return carry

    lax.fori_loop(1, NX, send_last, 0)

    def waiter(count, ref, one, two):
        whole = ref.at[pl.ds(0, count * CHUNK), :]
        return pltpu.make_async_remote_copy(
            src_ref=whole, dst_ref=whole, send_sem=one, recv_sem=two, device_id=(f, o), device_id_type=MESH
        )

    mom_in.wait()
    gram[...] = jnp.zeros_like(gram)

    def absorb(turn, count):
        waiter(count, recv, send_sem, recv_sem.at[turn]).wait_recv()
        z = (my_z + NZ - z_offset(turn)) % NZ

        def one_chunk(index, carry):
            x, k = index // ROW_SPLIT, index % ROW_SPLIT
            e, from_f, from_o = place(z, x, k)
            value = recv[chunk_of(e), :].astype(jnp.float32)
            first = (from_f * 2 + from_o) * CHUNK
            for j in range(BPG):
                grad = value[j * SUB : (j + 1) * SUB]
                rows = pl.ds(first + j, SUB, stride=BPG)
                new = decay_rate * mom[rows, :] + grad
                mom[rows, :] = new
                nest[j, pl.ds(pl.multiple_of(e * SUB, SUB), SUB), :] = grad + decay_rate * new
            return carry

        lax.fori_loop(0, BATCH, one_chunk, 0, unroll=4)
        for half in range(2):
            count_rows = ROW_SPLIT * NCORE * CHUNK
            rows = pl.ds(pl.multiple_of((half * NZ + z) * count_rows, count_rows), count_rows)
            pltpu.make_async_copy(mom.at[rows, :], new_hbm.at[rows, :], local_sems.at[1]).start()
        for j in range(BPG):
            x = nest[j, pl.ds(pl.multiple_of(z * BATCH * SUB, BATCH * SUB), BATCH * SUB), :]
            gram[j] += dot(x, x, left_dim=0)

    def absorb_turn(turn, carry):
        absorb(turn, BATCH)
        return carry

    lax.fori_loop(0, NZ - 1, absorb_turn, 0)
    absorb(NZ - 1, BATCH - 1)

    gram_in[my_k] = gram[my_y]
    for kk in range(1, ROW_SPLIT):
        k = target_k(kk)
        pltpu.make_async_remote_copy(
            src_ref=gram.at[k // 2],
            dst_ref=gram_in.at[my_k],
            send_sem=gram_sems.at[0],
            recv_sem=gram_sems.at[1],
            device_id=(f - my_k + k, o),
            device_id_type=MESH,
        ).start()
    seven = gram_in.at[pl.ds(0, ROW_SPLIT - 1)]
    pltpu.make_async_remote_copy(
        src_ref=seven,
        dst_ref=seven,
        send_sem=gram_sems.at[0],
        recv_sem=gram_sems.at[1],
        device_id=(f, o),
        device_id_type=MESH,
    ).wait()

    now = gram_in[0]
    for k in range(1, ROW_SPLIT):
        now = now + gram_in[k]
    eye = jnp.where(
        lax.broadcasted_iota(jnp.int32, (HD, HD), 0) == lax.broadcasted_iota(jnp.int32, (HD, HD), 1), 1.0, 0.0
    )
    inverse = 1.0 / (jnp.sqrt(jnp.sum(now * eye, axis=(0, 1), keepdims=True)) + epsilon)
    now = now * inverse * inverse
    total = None
    for step in range(ITERS):
        factor = first_coeff * eye + second_coeff * now + third_coeff * dot(now, now)
        total = factor if total is None else dot(total, factor)
        if step < ITERS - 1:
            now = dot(factor, dot(now, factor))
    chain[my_y] = total * (gain_factor * math.sqrt(max(D, HD)) * inverse)
    for dy in range(1, NY):
        y = (my_y + dy) % NY
        pltpu.make_async_remote_copy(
            src_ref=chain.at[my_y],
            dst_ref=chain.at[my_y],
            send_sem=chain_sems.at[0],
            recv_sem=chain_sems.at[1],
            device_id=(f - my_k + y * 2 + my_core, o),
            device_id_type=MESH,
        ).start()
    three = gram_in.at[pl.ds(0, NY - 1)]
    pltpu.make_async_remote_copy(
        src_ref=three,
        dst_ref=three,
        send_sem=chain_sems.at[0],
        recv_sem=chain_sems.at[1],
        device_id=(f, o),
        device_id_type=MESH,
    ).wait()

    def finish(turn, own):
        z = (my_z + z_offset(turn)) % NZ
        parts = []
        for j in range(BPG):
            x = nest[j, pl.ds(pl.multiple_of(z * BATCH * SUB, BATCH * SUB), BATCH * SUB), :]
            parts.append(dot(x, chain[j]).reshape(BATCH, SUB, HD))
        rows = pl.ds(pl.multiple_of(z * BATCH * CHUNK, BATCH * CHUNK), BATCH * CHUNK)
        back[rows, :] = jnp.stack(parts, axis=1).reshape(BATCH * CHUNK, HD).astype(jnp.bfloat16)

        def give(x, k):
            e, to_f, to_o = place(z, x, k)
            pltpu.make_async_remote_copy(
                src_ref=back.at[chunk_of(e), :],
                dst_ref=ret_hbm.at[chunk_of(my_e), :],
                send_sem=back_send_sem,
                recv_sem=back_recv_sem,
                device_id=(to_f, to_o),
                device_id_type=MESH,
            ).start()

        def give_turn(index, carry):
            kk = index // NX
            give((my_x + index % NX) % NX, target_k(kk))
            return carry

        if own:
            pltpu.make_async_copy(
                back.at[chunk_of(my_e), :], ret_hbm.at[chunk_of(my_e), :], local_sems.at[2]
            ).start()
        lax.fori_loop(1 if own else 0, BATCH, give_turn, 0)

    def finish_turn(turn, carry):
        finish(turn, False)
        return carry

    lax.fori_loop(0, NZ - 1, finish_turn, 0)
    finish(NZ - 1, True)

    pltpu.make_async_copy(mom, new_hbm, local_sems.at[1]).wait()
    pltpu.make_async_copy(back.at[chunk_of(my_e), :], ret_hbm.at[chunk_of(my_e), :], local_sems.at[2]).wait()
    waiter(NDEV - 1, send, send_sem, send_sem).wait_send()
    waiter(NDEV - 1, ret_hbm, back_send_sem, back_recv_sem).wait()


def place_kernel(order_ref, ret_ref, out_ref, wide, stage):
    def widen(index, carry):
        rows = pl.ds(pl.multiple_of(index * 128, 128), 128)
        wide[rows, :] = ret_ref[rows, :].astype(jnp.float32)
        return carry

    lax.fori_loop(0, ROWS // 128, widen, 0)

    def column(p, carry):
        block = order_ref[p]
        j, group = block % BPG, block // BPG
        x, z = (group // 16) * 2 + (group // NZ) % 2, group % NZ
        for k in range(ROW_SPLIT):
            e, _, _ = place(z, x, k)
            stage[pl.ds(k, SUB, stride=ROW_SPLIT), :] = wide[pl.ds(pl.multiple_of(e * CHUNK + j * SUB, SUB), SUB), :]
        out_ref[:, pl.ds(pl.multiple_of(p * HD, HD), HD)] = stage[...].astype(jnp.bfloat16)
        return carry

    lax.fori_loop(0, order_ref.shape[0], column, 0, unroll=2)


def per_device(gradient, momentum, head_order):
    blocks = head_order.shape[0]
    positions = jnp.arange(blocks, dtype=jnp.int32)
    source_of = jnp.sum(
        jnp.where(head_order[:, None] == positions[None, :], positions[:, None], 0), axis=0
    )
    vmem, smem, hbm = (pl.BlockSpec(memory_space=m) for m in (pltpu.VMEM, pltpu.SMEM, pl.ANY))
    returned, new = pl.pallas_call(
        kernel,
        out_shape=(
            jax.ShapeDtypeStruct((ROWS, HD), jnp.bfloat16),
            jax.ShapeDtypeStruct((ROWS, HD), jnp.float32),
        ),
        in_specs=[smem, vmem, hbm],
        out_specs=(hbm, hbm),
        scratch_shapes=[
            pltpu.VMEM((ROWS, HD), jnp.float32),
            pltpu.VMEM((ROWS, HD), jnp.bfloat16),
            pltpu.VMEM((ROWS, HD), jnp.bfloat16),
            pltpu.VMEM((BPG, NDEV * SUB, HD), jnp.float32),
            pltpu.VMEM((ROWS, HD), jnp.bfloat16),
            pltpu.VMEM((BPG, SUB * ROW_SPLIT, HD), jnp.float32),
            pltpu.VMEM((BPG, HD, HD), jnp.float32),
            pltpu.VMEM((ROW_SPLIT, HD, HD), jnp.float32),
            pltpu.VMEM((BPG, HD, HD), jnp.float32),
            pltpu.SemaphoreType.DMA,
            pltpu.SemaphoreType.DMA((NZ,)),
            pltpu.SemaphoreType.DMA,
            pltpu.SemaphoreType.DMA,
            pltpu.SemaphoreType.DMA((2,)),
            pltpu.SemaphoreType.DMA((2,)),
            pltpu.SemaphoreType.DMA((3,)),
        ],
        compiler_params=pltpu.CompilerParams(has_side_effects=True, vmem_limit_bytes=56 * 2**20),
    )(source_of, gradient, momentum.reshape(ROWS, HD))
    placed = pl.pallas_call(
        place_kernel,
        out_shape=jax.ShapeDtypeStruct(gradient.shape, jnp.bfloat16),
        in_specs=[smem, vmem],
        out_specs=vmem,
        scratch_shapes=[
            pltpu.VMEM((ROWS, HD), jnp.float32),
            pltpu.VMEM((SUB * ROW_SPLIT, HD), jnp.float32),
        ],
        compiler_params=pltpu.CompilerParams(vmem_limit_bytes=32 * 2**20),
    )(head_order, returned)
    return (placed, new.reshape(momentum.shape))


def solution(mesh):
    in_specs = (P(("fsdp", "opt"), None), P("fsdp", "opt", None, None, None), P())
    out_specs = (P(("fsdp", "opt"), None), P("fsdp", "opt", None, None, None))
    return jax.shard_map(
        per_device, mesh=mesh, in_specs=in_specs, out_specs=out_specs, check_vma=False
    )
```

time: 208 us -> 152 us (0.73)
  Pallas kernels: 0 us -> 146 us
  blocking collectives: 68.6 us -> 0 us
  waiting for transfers between devices: 56.4 us -> 0 us
  local copies, waits for them, and re-layouts: 33.8 us -> 3.61 us
  matrix products: 18.6 us -> 0 us
  other arithmetic: 16.3 us -> 1.33 us
  starting transfers between devices: 12.6 us -> 0 us
    pallas_call x0 -> x2, Pallas kernels: none -> 146 us  [the longest x1 140 us: per_device(): pl.pallas_call(kernel, out_shape=(jax.ShapeDtypeStruct((ROWS, HD), jnp.bf...]
    all_to_all x1 -> x0, blocking collectives: 68.6 us -> none  [per_device(): lax.all_to_all(sectioned, ('fsdp', 'opt'), split_axis=0, concat_axis=0, t...]
    all_to_all x1 -> x0, waiting for transfers between devices: 41.9 us -> none  [per_device(): lax.all_to_all(outgoing, ('fsdp', 'opt'), split_axis=0, concat_axis=0, ti...]
    dot_general x19 -> x0, matrix products: 18.6 us -> none  [the longest x1 6.81 us: local_gram(): jnp.einsum('rjc,rjd->jcd', values, values, precision=lax.Precision.HIGHEST)]
    ppermute x3 -> x0, waiting for transfers between devices: 14.5 us -> none  [partner(): return lax.ppermute(value, axis, pairs)]
    convert_element_type x3 -> x0, local copies, waits for them, and re-layouts: 13.7 us -> none  [the longest x2 9.43 us: per_device(): local_grad = arrived.reshape(-1, BPG, head_size).astype(jnp.float32)]
    reshape x4 -> x0, local copies, waits for them, and re-layouts: 12 us -> none  [the longest x1 5.34 us: per_device(): returned.reshape(groups, ROW_SPLIT, opt_size, inner, BPG, head_size)]
    add x4 -> x0, other arithmetic: 9.96 us -> none  [the longest x1 5.51 us: per_device(): new_state = decay_rate * previous + local_grad]
  transfers between devices with their start and end apart: 4 -> 0, of which waited for: 4 -> 0; matrix products, arithmetic and copies ran while one was open for 5% -> 0% of each run, Pallas kernels for 0% -> 0%
where the time goes in v2:
time: 152 us
  Pallas kernels  146 us (96%)
  local copies, waits for them, and re-layouts  3.61 us (2%)
    pallas_call x1, Pallas kernels, per_device(): pl.pallas_call(kernel, out_shape=(jax.ShapeDtypeStruct((ROWS, HD), jnp.bf...  140 us
    pallas_call x1, Pallas kernels, per_device(): pl.pallas_call(place_kernel, out_shape=jax.ShapeDtypeStruct(gradient.shap...  5.84 us
    unnamed x7, local copies, waits for them, and re-layouts  3.61 us

profile of v2, /device:TPU:1, one launch (start us, length us, event | category | flops | bytes accessed | tf_op | source)
XLA Modules:
  0.0 151.6 jit_solution(3660413002139096633)
XLA Ops:
  0.6 0.0 copy-start.1
  0.6 1.3 select_reduce_fusion.source_ref
  2.0 140.2 %shard_map.50 = (bf16[8192,128]{1,0:T(8,128)(2,1)}, f32[8192,128]{1,0:T(8,128)}) custom-call(s32[128]{0:T(128)} %select_reduce_fusion.source_ref, bf16[64,16384]{1,0:T(8,128)(2,1)} %grad_ref.1, f32[8192,128]{1,0:T(8,128)} %bitcast.2), custom_call_target="tpu_custom_call" | custom-call | tf_op jit(solution)/shard_map/pallas_call | solution.py:296
  142.2 0.0 copy-done.1
  142.2 0.0 copy-start
  142.2 1.6 %copy-done = bf16[8192,128]{1,0:T(8,128)(2,1)S(1)} copy-done((bf16[8192,128]{1,0:T(8,128)(2,1)S(1)}, bf16[8192,128]{1,0:T(8,128)(2,1)}, u32[]{:S(2)}) %copy-start) | copy-done | bytes 2097176
  143.8 0.0 copy-start.2
  143.8 5.8 %shard_map.51 = bf16[64,16384]{1,0:T(8,128)(2,1)} custom-call(s32[128]{0:T(128)S(1)} %copy-done.1, bf16[8192,128]{1,0:T(8,128)(2,1)S(1)} %copy-done), custom_call_target="tpu_custom_call" | custom-call | tf_op jit(solution)/shard_map/pallas_call | solution.py:324
  149.6 0.0 copy-done.2
  149.6 2.0 %copy.6 = f32[1,1,2048,4,128]{4,3,2,1,0:T(4,128)} copy(f32[1,1,2048,4,128]{4,3,2,1,0:T(4,128)S(1)} %bitcast.3) | data formatting | bytes 8388608
Async XLA Ops:
  0.6 141.5 %copy-start.1 = (s32[128]{0:T(128)S(1)}, s32[128]{0:T(128)}, u32[]{:S(2)}) copy-start(s32[128]{0:T(128)} %order_ref.1) | copy-start | bytes 1540
  142.2 1.6 %copy-start = (bf16[8192,128]{1,0:T(8,128)(2,1)S(1)}, bf16[8192,128]{1,0:T(8,128)(2,1)}, u32[]{:S(2)}) copy-start(bf16[8192,128]{1,0:T(8,128)(2,1)} %get-tuple-element.4.ret_ref) | copy-start | bytes 6291460
  143.8 5.8 %copy-start.2 = (f32[8192,128]{1,0:T(8,128)S(1)}, f32[8192,128]{1,0:T(8,128)}, u32[]{:S(2)}) copy-start(f32[8192,128]{1,0:T(8,128)} %get-tuple-element.5) | copy-start | bytes 12582916

commit v3 on v1

v3 whole, which is shorter than its diff:
```python
import math

import jax
import jax.numpy as jnp
from jax import lax
from jax.experimental import pallas as pl
from jax.experimental.pallas import tpu as pltpu
from jax.sharding import PartitionSpec as P

D = 16384
HD = 128
BPG = 4
ROW_SPLIT = 8
ITERS = 5
NX, NY, NZ, NCORE = 4, 4, 8, 2
NDEV = NX * NY * NZ * NCORE
SUB = 8
HALF = BPG // 2
CHUNK = SUB * HALF
BATCH = NX * ROW_SPLIT
ROWS = 2 * NDEV * CHUNK

decay_rate = 0.95
first_coeff = 3.4445
second_coeff = -4.775
third_coeff = 2.0315
epsilon = 1e-07
gain_factor = 0.2

MESH = pl.DeviceIdType.MESH
HIGHEST = lax.Precision.HIGHEST


def dot(left, right, left_dim=1):
    return lax.dot_general(
        left, right, (((left_dim,), (0,)), ((), ())), precision=HIGHEST, preferred_element_type=jnp.float32
    )


def z_offset(turn):
    back = NZ - 1 - turn
    odd = back % 2
    return odd * ((back + 1) // 2) + (1 - odd) * ((NZ - back // 2) % NZ)


def place(z, x, k):
    return (z * NX + x) * ROW_SPLIT + k, ((x % 2) * NZ + z) * ROW_SPLIT + k, x // 2


def chunk_of(index):
    return pl.ds(pl.multiple_of(index * CHUNK, CHUNK), CHUNK)


def kernel(
    source_ref,
    grad_ref,
    mom_hbm,
    ret_hbm,
    new_hbm,
    mom,
    send,
    recv,
    nest,
    back,
    stage,
    gram,
    pair_in,
    ring_in,
    chain,
    send_sem,
    recv_sem,
    back_sems,
    pair_sems,
    ring_sems,
    chain_sems,
    local_sems,
):
    f, o = lax.axis_index("fsdp"), lax.axis_index("opt")
    my_k = f % ROW_SPLIT
    my_z = (f // ROW_SPLIT) % NZ
    my_x = o * 2 + f // (ROW_SPLIT * NZ)
    my_y, my_core = my_k // 2, my_k % 2
    my_e, _, _ = place(my_z, my_x, my_k)

    mom_in = pltpu.make_async_copy(mom_hbm, mom, local_sems.at[0])
    mom_in.start()

    barrier = pltpu.get_barrier_semaphore()

    def greet(index, carry):
        other = (f * 2 + o + index) % NDEV
        pl.semaphore_signal(barrier, inc=1, device_id=(other // 2, other % 2), device_id_type=MESH)
        return carry

    lax.fori_loop(1, NDEV, greet, 0)
    gram[...] = jnp.zeros_like(gram)
    pl.semaphore_wait(barrier, NDEV - 1)

    def target_k(kk):
        return ((my_y + kk // 2) % NY) * 2 + (my_core + kk % 2) % 2

    def remote(src, dst, one, two, to):
        return pltpu.make_async_remote_copy(
            src_ref=src, dst_ref=dst, send_sem=one, recv_sem=two, device_id=to, device_id_type=MESH
        )

    def give(src, dst, one, two, e, to):
        @pl.when(e != my_e)
        def _():
            remote(src, dst, one, two, to).start()

        @pl.when(e == my_e)
        def _():
            pltpu.make_async_copy(src, dst, two).start()

    def send_turns(h, first, last):
        def send_group(index, carry):
            turn, r = index // NX, index % NX
            z, x = (my_z + z_offset(turn)) % NZ, (my_x + r) % NX
            group = (x // 2) * 16 + (x % 2) * NZ + z
            for j in range(HALF):
                column = source_ref[group * BPG + h * HALF + j] * HD
                stage[j] = grad_ref[:, pl.ds(column, HD)].astype(jnp.float32)
            for kk in range(ROW_SPLIT):
                k = target_k(kk)
                e, to_f, to_o = place(z, x, k)
                parts = [stage[j, pl.ds(k, SUB, stride=ROW_SPLIT), :] for j in range(HALF)]
                send[chunk_of(h * NDEV + e), :] = jnp.concatenate(parts, axis=0).astype(jnp.bfloat16)
                src, dst = send.at[chunk_of(h * NDEV + e), :], recv.at[chunk_of(h * NDEV + my_e), :]
                if kk:
                    remote(src, dst, send_sem, recv_sem.at[h, turn], (to_f, to_o)).start()
                else:
                    give(src, dst, send_sem, recv_sem.at[h, turn], e, (to_f, to_o))
            return carry

        lax.fori_loop(first * NX, last * NX, send_group, 0)

    def absorb_turns(h, first, last):
        def absorb(turn, carry):
            whole = recv.at[pl.ds(0, BATCH * CHUNK), :]
            remote(whole, whole, send_sem, recv_sem.at[h, turn], (f, o)).wait_recv()
            z = (my_z + NZ - z_offset(turn)) % NZ

            def one_chunk(index, carry):
                x, k = index // ROW_SPLIT, index % ROW_SPLIT
                e, from_f, from_o = place(z, x, k)
                value = recv[chunk_of(h * NDEV + e), :].astype(jnp.float32)
                start = (from_f * 2 + from_o) * SUB * BPG
                for j in range(HALF):
                    grad = value[j * SUB : (j + 1) * SUB]
                    rows = pl.ds(start + h * HALF + j, SUB, stride=BPG)
                    new = decay_rate * mom[rows, :] + grad
                    mom[rows, :] = new
                    nest[h * HALF + j, pl.ds(pl.multiple_of(e * SUB, SUB), SUB), :] = grad + decay_rate * new
                return carry

            lax.fori_loop(0, BATCH, one_chunk, 0, unroll=4)
            if h:
                for side in range(2):
                    count = ROW_SPLIT * NCORE * SUB * BPG
                    rows = pl.ds(pl.multiple_of((side * NZ + z) * count, count), count)
                    pltpu.make_async_copy(mom.at[rows, :], new_hbm.at[rows, :], local_sems.at[1]).start()
            for j in range(HALF):
                x = nest[h * HALF + j, pl.ds(pl.multiple_of(z * BATCH * SUB, BATCH * SUB), BATCH * SUB), :]
                gram[h * HALF + j] += dot(x, x, left_dim=0)
            return carry

        lax.fori_loop(first, last, absorb, 0)

    sibling = (f + 1 - 2 * my_core, o)

    def pair_copy(h):
        return remote(
            gram.at[h * HALF + 1 - my_core], pair_in.at[h], pair_sems.at[0, h], pair_sems.at[1, h], sibling
        )

    def ring_start(h):
        pair_copy(h).wait()
        ring_in[h * NY + my_y] = gram[h * HALF + my_core] + pair_in[h]
        for dy in range(1, NY):
            piece = ring_in.at[h * NY + my_y]
            to_f = f - my_k + ((my_y + dy) % NY) * 2 + my_core
            remote(piece, piece, ring_sems.at[0, h], ring_sems.at[1, h], (to_f, o)).start()

    def chain_copy(h):
        piece = chain.at[h * HALF + my_core]
        return remote(piece, piece, chain_sems.at[0, h], chain_sems.at[1, h], sibling)

    def factors(h):
        three = ring_in.at[pl.ds(0, NY - 1)]
        remote(three, three, ring_sems.at[0, h], ring_sems.at[1, h], (f, o)).wait()
        now = ring_in[h * NY]
        for y in range(1, NY):
            now = now + ring_in[h * NY + y]
        rows, columns = (lax.broadcasted_iota(jnp.int32, (HD, HD), d) for d in range(2))
        eye = jnp.where(rows == columns, 1.0, 0.0)
        inverse = 1.0 / (jnp.sqrt(jnp.sum(now * eye, axis=(0, 1), keepdims=True)) + epsilon)
        now = now * inverse * inverse
        total = None
        for step in range(ITERS):
            factor = first_coeff * eye + second_coeff * now + third_coeff * dot(now, now)
            total = factor if total is None else dot(total, factor)
            if step < ITERS - 1:
                now = dot(factor, dot(now, factor))
        chain[h * HALF + my_core] = total * (gain_factor * math.sqrt(max(D, HD)) * inverse)
        chain_copy(h).start()

    def finish_turns(h, first, last):
        def finish(turn, carry):
            z = (my_z + z_offset(turn)) % NZ
            parts = []
            for j in range(HALF):
                x = nest[h * HALF + j, pl.ds(pl.multiple_of(z * BATCH * SUB, BATCH * SUB), BATCH * SUB), :]
                parts.append(dot(x, chain[h * HALF + j]).reshape(BATCH, SUB, HD))
            rows = pl.ds(pl.multiple_of((h * NZ + z) * BATCH * CHUNK, BATCH * CHUNK), BATCH * CHUNK)
            back[rows, :] = jnp.stack(parts, axis=1).reshape(BATCH * CHUNK, HD).astype(jnp.bfloat16)

            def give_turn(index, carry):
                x = (my_x + index % NX) % NX
                e, to_f, to_o = place(z, x, target_k(index // NX))
                src, dst = back.at[chunk_of(h * NDEV + e), :], ret_hbm.at[chunk_of(h * NDEV + my_e), :]
                give(src, dst, back_sems.at[0], back_sems.at[1], e, (to_f, to_o))
                return carry

            lax.fori_loop(0, BATCH, give_turn, 0)
            return carry

        lax.fori_loop(first, last, finish, 0)

    send_turns(0, 0, NZ)
    mom_in.wait()
    absorb_turns(0, 0, 6)
    send_turns(1, 0, 2)
    absorb_turns(0, 6, NZ)
    pair_copy(0).start()
    send_turns(1, 2, 3)
    ring_start(0)
    send_turns(1, 3, NZ)
    factors(0)
    absorb_turns(1, 0, 6)
    chain_copy(0).wait()
    finish_turns(0, 0, 2)
    absorb_turns(1, 6, NZ)
    pair_copy(1).start()
    finish_turns(0, 2, 3)
    ring_start(1)
    finish_turns(0, 3, 6)
    factors(1)
    finish_turns(0, 6, NZ)
    chain_copy(1).wait()
    finish_turns(1, 0, NZ)

    pltpu.make_async_copy(mom, new_hbm, local_sems.at[1]).wait()
    sent = send.at[pl.ds(0, 2 * (NDEV - 1) * CHUNK), :]
    remote(sent, sent, send_sem, send_sem, (f, o)).wait_send()
    remote(sent, sent, back_sems.at[0], back_sems.at[0], (f, o)).wait_send()
    remote(ret_hbm, ret_hbm, back_sems.at[0], back_sems.at[1], (f, o)).wait_recv()


LANES = 4


def place_kernel(order_ref, ret_ref, out_ref, wide, stage):
    def widen(index, carry):
        rows = pl.ds(pl.multiple_of(index * 128, 128), 128)
        wide[rows, :] = ret_ref[rows, :].astype(jnp.float32)
        return carry

    lax.fori_loop(0, ROWS // 128, widen, 0, unroll=2)

    def columns(index, carry):
        for lane in range(LANES):
            p = index * LANES + lane
            block = order_ref[p]
            j, group = block % BPG, block // BPG
            x, z = (group // 16) * 2 + (group // NZ) % 2, group % NZ
            first = ((j // HALF) * NDEV + (z * NX + x) * ROW_SPLIT) * CHUNK + (j % HALF) * SUB
            for k in range(ROW_SPLIT):
                rows = pl.ds(pl.multiple_of(first + k * CHUNK, SUB), SUB)
                stage[lane, pl.ds(k, SUB, stride=ROW_SPLIT), :] = wide[rows, :]
        for lane in range(LANES):
            p = index * LANES + lane
            out_ref[:, pl.ds(pl.multiple_of(p * HD, HD), HD)] = stage[lane].astype(jnp.bfloat16)
        return carry

    lax.fori_loop(0, order_ref.shape[0] // LANES, columns, 0)


def per_device(gradient, momentum, head_order):
    blocks = head_order.shape[0]
    positions = jnp.arange(blocks, dtype=jnp.int32)
    source_of = jnp.sum(
        jnp.where(head_order[:, None] == positions[None, :], positions[:, None], 0), axis=0
    )
    vmem, smem, hbm = (pl.BlockSpec(memory_space=m) for m in (pltpu.VMEM, pltpu.SMEM, pl.ANY))
    returned, new = pl.pallas_call(
        kernel,
        out_shape=(
            jax.ShapeDtypeStruct((ROWS, HD), jnp.bfloat16),
            jax.ShapeDtypeStruct((ROWS, HD), jnp.float32),
        ),
        in_specs=[smem, vmem, hbm],
        out_specs=(hbm, hbm),
        scratch_shapes=[
            pltpu.VMEM((ROWS, HD), jnp.float32),
            pltpu.VMEM((ROWS, HD), jnp.bfloat16),
            pltpu.VMEM((ROWS, HD), jnp.bfloat16),
            pltpu.VMEM((BPG, NDEV * SUB, HD), jnp.float32),
            pltpu.VMEM((ROWS, HD), jnp.bfloat16),
            pltpu.VMEM((HALF, SUB * ROW_SPLIT, HD), jnp.float32),
            pltpu.VMEM((BPG, HD, HD), jnp.float32),
            pltpu.VMEM((2, HD, HD), jnp.float32),
            pltpu.VMEM((2 * NY, HD, HD), jnp.float32),
            pltpu.VMEM((BPG, HD, HD), jnp.float32),
            pltpu.SemaphoreType.DMA,
            pltpu.SemaphoreType.DMA((2, NZ)),
            pltpu.SemaphoreType.DMA((2,)),
            pltpu.SemaphoreType.DMA((2, 2)),
            pltpu.SemaphoreType.DMA((2, 2)),
            pltpu.SemaphoreType.DMA((2, 2)),
            pltpu.SemaphoreType.DMA((2,)),
        ],
        compiler_params=pltpu.CompilerParams(
            collective_id=0, has_side_effects=True, vmem_limit_bytes=56 * 2**20
        ),
    )(source_of, gradient, momentum.reshape(ROWS, HD))
    placed = pl.pallas_call(
        place_kernel,
        out_shape=jax.ShapeDtypeStruct(gradient.shape, jnp.bfloat16),
        in_specs=[smem, vmem],
        out_specs=vmem,
        scratch_shapes=[
            pltpu.VMEM((ROWS, HD), jnp.float32),
            pltpu.VMEM((LANES, SUB * ROW_SPLIT, HD), jnp.float32),
        ],
        compiler_params=pltpu.CompilerParams(vmem_limit_bytes=32 * 2**20),
    )(head_order, returned)
    return (placed, new.reshape(momentum.shape))


def solution(mesh):
    in_specs = (P(("fsdp", "opt"), None), P("fsdp", "opt", None, None, None), P())
    out_specs = (P(("fsdp", "opt"), None), P("fsdp", "opt", None, None, None))
    return jax.shard_map(
        per_device, mesh=mesh, in_specs=in_specs, out_specs=out_specs, check_vma=False
    )
```

time: 208 us -> 138 us (0.66)
  Pallas kernels: 0 us -> 133 us
  blocking collectives: 68.6 us -> 0 us
  waiting for transfers between devices: 56.4 us -> 0 us
  local copies, waits for them, and re-layouts: 33.8 us -> 3.61 us
  matrix products: 18.6 us -> 0 us
  other arithmetic: 16.3 us -> 1.33 us
  starting transfers between devices: 12.6 us -> 0 us
    pallas_call x0 -> x2, Pallas kernels: none -> 133 us  [the longest x1 126 us: per_device(): pl.pallas_call(kernel, out_shape=(jax.ShapeDtypeStruct((ROWS, HD), jnp.bf...]
    all_to_all x1 -> x0, blocking collectives: 68.6 us -> none  [per_device(): lax.all_to_all(sectioned, ('fsdp', 'opt'), split_axis=0, concat_axis=0, t...]
    all_to_all x1 -> x0, waiting for transfers between devices: 41.9 us -> none  [per_device(): lax.all_to_all(outgoing, ('fsdp', 'opt'), split_axis=0, concat_axis=0, ti...]
    dot_general x19 -> x0, matrix products: 18.6 us -> none  [the longest x1 6.81 us: local_gram(): jnp.einsum('rjc,rjd->jcd', values, values, precision=lax.Precision.HIGHEST)]
    ppermute x3 -> x0, waiting for transfers between devices: 14.5 us -> none  [partner(): return lax.ppermute(value, axis, pairs)]
    convert_element_type x3 -> x0, local copies, waits for them, and re-layouts: 13.7 us -> none  [the longest x2 9.43 us: per_device(): local_grad = arrived.reshape(-1, BPG, head_size).astype(jnp.float32)]
    reshape x4 -> x0, local copies, waits for them, and re-layouts: 12 us -> none  [the longest x1 5.34 us: per_device(): returned.reshape(groups, ROW_SPLIT, opt_size, inner, BPG, head_size)]
    add x4 -> x0, other arithmetic: 9.96 us -> none  [the longest x1 5.51 us: per_device(): new_state = decay_rate * previous + local_grad]
  transfers between devices with their start and end apart: 4 -> 0, of which waited for: 4 -> 0; matrix products, arithmetic and copies ran while one was open for 5% -> 0% of each run, Pallas kernels for 0% -> 0%
where the time goes in v3:
time: 138 us
  Pallas kernels  133 us (96%)
  local copies, waits for them, and re-layouts  3.61 us (3%)
    pallas_call x1, Pallas kernels, per_device(): pl.pallas_call(kernel, out_shape=(jax.ShapeDtypeStruct((ROWS, HD), jnp.bf...  126 us
    pallas_call x1, Pallas kernels, per_device(): pl.pallas_call(place_kernel, out_shape=jax.ShapeDtypeStruct(gradient.shap...  6.14 us
    unnamed x7, local copies, waits for them, and re-layouts  3.61 us

profile of v3, /device:TPU:1, one launch (start us, length us, event | category | flops | bytes accessed | tf_op | source)
XLA Modules:
  0.0 138.1 jit_solution(13187512756709850945)
XLA Ops:
  0.6 0.0 copy-start.1
  0.6 1.3 select_reduce_fusion.source_ref
  2.0 126.4 %shard_map.50 = (bf16[8192,128]{1,0:T(8,128)(2,1)}, f32[8192,128]{1,0:T(8,128)}) custom-call(s32[128]{0:T(128)} %select_reduce_fusion.source_ref, bf16[64,16384]{1,0:T(8,128)(2,1)} %grad_ref.1, f32[8192,128]{1,0:T(8,128)} %bitcast.2), custom_call_target="tpu_custom_call" | custom-call | tf_op jit(solution)/shard_map/pallas_call | solution.py:296
  128.3 0.0 copy-done.1
  128.3 0.0 copy-start
  128.4 1.6 %copy-done = bf16[8192,128]{1,0:T(8,128)(2,1)S(1)} copy-done((bf16[8192,128]{1,0:T(8,128)(2,1)S(1)}, bf16[8192,128]{1,0:T(8,128)(2,1)}, u32[]{:S(2)}) %copy-start) | copy-done | bytes 2097176
  129.9 0.0 copy-start.2
  129.9 6.1 %shard_map.51 = bf16[64,16384]{1,0:T(8,128)(2,1)} custom-call(s32[128]{0:T(128)S(1)} %copy-done.1, bf16[8192,128]{1,0:T(8,128)(2,1)S(1)} %copy-done), custom_call_target="tpu_custom_call" | custom-call | tf_op jit(solution)/shard_map/pallas_call | solution.py:327
  136.1 0.0 copy-done.2
  136.1 2.0 %copy.6 = f32[1,1,2048,4,128]{4,3,2,1,0:T(4,128)} copy(f32[1,1,2048,4,128]{4,3,2,1,0:T(4,128)S(1)} %bitcast.3) | data formatting | bytes 8388608
Async XLA Ops:
  0.6 127.7 %copy-start.1 = (s32[128]{0:T(128)S(1)}, s32[128]{0:T(128)}, u32[]{:S(2)}) copy-start(s32[128]{0:T(128)} %order_ref.1) | copy-start | bytes 1540
  128.3 1.6 %copy-start = (bf16[8192,128]{1,0:T(8,128)(2,1)S(1)}, bf16[8192,128]{1,0:T(8,128)(2,1)}, u32[]{:S(2)}) copy-start(bf16[8192,128]{1,0:T(8,128)(2,1)} %get-tuple-element.4.ret_ref) | copy-start | bytes 6291460
  129.9 6.1 %copy-start.2 = (f32[8192,128]{1,0:T(8,128)S(1)}, f32[8192,128]{1,0:T(8,128)}, u32[]{:S(2)}) copy-start(f32[8192,128]{1,0:T(8,128)} %get-tuple-element.5) | copy-start | bytes 12582916

commit v4 on v3

--- a/solution.py
+++ b/solution.py
@@ -87,14 +87,43 @@
 
     barrier = pltpu.get_barrier_semaphore()
 
-    def greet(index, carry):
-        other = (f * 2 + o + index) % NDEV
-        pl.semaphore_signal(barrier, inc=1, device_id=(other // 2, other % 2), device_id_type=MESH)
-        return carry
-
-    lax.fori_loop(1, NDEV, greet, 0)
+    leader = (my_k == 0) & (o == 0)
+    root = leader & (f == 0)
+    groups, members = NX * NZ // 2, 2 * ROW_SPLIT
+
+    def signal(to):
+        pl.semaphore_signal(barrier, inc=1, device_id=to, device_id_type=MESH)
+
+    @pl.when(jnp.logical_not(leader))
+    def _():
+        signal((f - my_k, 0))
+        pl.semaphore_wait(barrier, 1)
+
+    @pl.when(leader & (f != 0))
+    def _():
+        pl.semaphore_wait(barrier, members - 1)
+        signal((0, 0))
+        pl.semaphore_wait(barrier, 1)
+
+    @pl.when(root)
+    def _():
+        pl.semaphore_wait(barrier, groups + members - 2)
+
+        def to_leader(group, carry):
+            signal((group * ROW_SPLIT, 0))
+            return carry
+
+        lax.fori_loop(1, groups, to_leader, 0)
+
+    @pl.when(leader)
+    def _():
+        def to_member(index, carry):
+            signal((f + index // 2, index % 2))
+            return carry
+
+        lax.fori_loop(1, members, to_member, 0)
+
     gram[...] = jnp.zeros_like(gram)
-    pl.semaphore_wait(barrier, NDEV - 1)
 
     def target_k(kk):
         return ((my_y + kk // 2) % NY) * 2 + (my_core + kk % 2) % 2
@@ -257,33 +286,49 @@
     remote(ret_hbm, ret_hbm, back_sems.at[0], back_sems.at[1], (f, o)).wait_recv()
 
 
-LANES = 4
-
-
-def place_kernel(order_ref, ret_ref, out_ref, wide, stage):
-    def widen(index, carry):
-        rows = pl.ds(pl.multiple_of(index * 128, 128), 128)
-        wide[rows, :] = ret_ref[rows, :].astype(jnp.float32)
-        return carry
-
-    lax.fori_loop(0, ROWS // 128, widen, 0, unroll=2)
-
-    def columns(index, carry):
-        for lane in range(LANES):
-            p = index * LANES + lane
+PIECES = 8
+
+
+def place_kernel(order_ref, ret_hbm, new_hbm, out_hbm, kept_hbm, ret, wide, out, kept, in_sems, out_sems):
+    rows_of = [pl.ds(i * (ROWS // PIECES), ROWS // PIECES) for i in range(PIECES)]
+    for i, rows in enumerate(rows_of):
+        pltpu.make_async_copy(ret_hbm.at[rows, :], ret.at[rows, :], in_sems.at[i]).start()
+    for rows in rows_of:
+        pltpu.make_async_copy(new_hbm.at[rows, :], kept.at[rows, :], out_sems.at[0]).start()
+
+    for i, rows in enumerate(rows_of):
+        pltpu.make_async_copy(ret_hbm.at[rows, :], ret.at[rows, :], in_sems.at[i]).wait()
+
+        def widen(index, carry):
+            some = pl.ds(pl.multiple_of(i * (ROWS // PIECES) + index * 128, 128), 128)
+            wide[some, :] = ret[some, :].astype(jnp.float32)
+            return carry
+
+        lax.fori_loop(0, ROWS // PIECES // 128, widen, 0, unroll=2)
+
+    pltpu.make_async_copy(new_hbm, kept, out_sems.at[0]).wait()
+    for rows in rows_of:
+        pltpu.make_async_copy(kept.at[rows, :], kept_hbm.at[rows, :], out_sems.at[1]).start()
+
+    columns = order_ref.shape[0] // PIECES
+    for i in range(PIECES):
+
+        def column(index, carry):
+            p = i * columns + index
             block = order_ref[p]
             j, group = block % BPG, block // BPG
             x, z = (group // 16) * 2 + (group // NZ) % 2, group % NZ
             first = ((j // HALF) * NDEV + (z * NX + x) * ROW_SPLIT) * CHUNK + (j % HALF) * SUB
-            for k in range(ROW_SPLIT):
-                rows = pl.ds(pl.multiple_of(first + k * CHUNK, SUB), SUB)
-                stage[lane, pl.ds(k, SUB, stride=ROW_SPLIT), :] = wide[rows, :]
-        for lane in range(LANES):
-            p = index * LANES + lane
-            out_ref[:, pl.ds(pl.multiple_of(p * HD, HD), HD)] = stage[lane].astype(jnp.bfloat16)
-        return carry
-
-    lax.fori_loop(0, order_ref.shape[0] // LANES, columns, 0)
+            tiles = [wide[pl.ds(first + row, ROW_SPLIT, stride=CHUNK), :] for row in range(SUB)]
+            out[:, pl.ds(pl.multiple_of(p * HD, HD), HD)] = jnp.concatenate(tiles, axis=0).astype(jnp.bfloat16)
+            return carry
+
+        lax.fori_loop(0, columns, column, 0, unroll=4)
+        panel = pl.ds(i * columns * HD, columns * HD)
+        pltpu.make_async_copy(out.at[:, panel], out_hbm.at[:, panel], out_sems.at[2]).start()
+
+    pltpu.make_async_copy(kept, kept_hbm, out_sems.at[1]).wait()
+    pltpu.make_async_copy(out, out_hbm, out_sems.at[2]).wait()
 
 
 def per_device(gradient, momentum, head_order):
@@ -324,18 +369,25 @@
             collective_id=0, has_side_effects=True, vmem_limit_bytes=56 * 2**20
         ),
     )(source_of, gradient, momentum.reshape(ROWS, HD))
-    placed = pl.pallas_call(
+    placed, kept = pl.pallas_call(
         place_kernel,
-        out_shape=jax.ShapeDtypeStruct(gradient.shape, jnp.bfloat16),
-        in_specs=[smem, vmem],
-        out_specs=vmem,
+        out_shape=(
+            jax.ShapeDtypeStruct(gradient.shape, jnp.bfloat16),
+            jax.ShapeDtypeStruct((ROWS, HD), jnp.float32),
+        ),
+        in_specs=[smem, hbm, hbm],
+        out_specs=(hbm, hbm),
         scratch_shapes=[
+            pltpu.VMEM((ROWS, HD), jnp.bfloat16),
             pltpu.VMEM((ROWS, HD), jnp.float32),
-            pltpu.VMEM((LANES, SUB * ROW_SPLIT, HD), jnp.float32),
+            pltpu.VMEM(gradient.shape, jnp.bfloat16),
+            pltpu.VMEM((ROWS, HD), jnp.float32),
+            pltpu.SemaphoreType.DMA((PIECES,)),
+            pltpu.SemaphoreType.DMA((3,)),
         ],
-        compiler_params=pltpu.CompilerParams(vmem_limit_bytes=32 * 2**20),
-    )(head_order, returned)
-    return (placed, new.reshape(momentum.shape))
+        compiler_params=pltpu.CompilerParams(vmem_limit_bytes=58 * 2**20),
+    )(head_order, returned, new)
+    return (placed, kept.reshape(momentum.shape))
 
 
 def solution(mesh):

time: 138 us -> 138 us (level)
  local copies, waits for them, and re-layouts: 3.61 us -> 0 us
  Pallas kernels: 133 us -> 135 us
    unnamed x7 -> x0, local copies, waits for them, and re-layouts: 3.61 us -> none
    pallas_call x1, Pallas kernels: 6.14 us -> 8.3 us  [per_device(): pl.pallas_call(place_kernel, out_shape=(jax.ShapeDtypeStruct(gradient.sha...]
where the time goes in v4:
time: 138 us; the launch traced here: 137 us
  Pallas kernels  135 us (98%)
    pallas_call x1, Pallas kernels, per_device(): pl.pallas_call(kernel, out_shape=(jax.ShapeDtypeStruct((ROWS, HD), jnp.bf...  127 us
    pallas_call x1, Pallas kernels, per_device(): pl.pallas_call(place_kernel, out_shape=(jax.ShapeDtypeStruct(gradient.sha...  8.3 us

profile of v4, /device:TPU:1, one launch (start us, length us, event | category | flops | bytes accessed | tf_op | source)
XLA Modules:
  0.0 137.4 jit_solution(15289019466186724032)
XLA Ops:
  0.6 1.3 select_reduce_fusion.source_ref
  1.9 127.2 %shard_map.50 = (bf16[8192,128]{1,0:T(8,128)(2,1)}, f32[8192,128]{1,0:T(8,128)}) custom-call(s32[128]{0:T(128)} %select_reduce_fusion.source_ref, bf16[64,16384]{1,0:T(8,128)(2,1)} %grad_ref.1, f32[8192,128]{1,0:T(8,128)} %bitcast.2), custom_call_target="tpu_custom_call" | custom-call | tf_op jit(solution)/shard_map/pallas_call | solution.py:341
  129.1 8.3 %shard_map.51 = (bf16[64,16384]{1,0:T(8,128)(2,1)}, f32[8192,128]{1,0:T(8,128)}) custom-call(s32[128]{0:T(128)} %order_ref.1, bf16[8192,128]{1,0:T(8,128)(2,1)} %get-tuple-element.6.ret_hbm, f32[8192,128]{1,0:T(8,128)} %get-tuple-element.7.new_hbm), custom_call_target="tpu_custom_call" | custom-call | tf_op jit(solution)/shard_map/pallas_call | solution.py:372

commit v5 on v4

--- a/solution.py
+++ b/solution.py
@@ -37,6 +37,16 @@
     )
 
 
+def split(value):
+    high = value.astype(jnp.bfloat16)
+    return high, (value - high.astype(jnp.float32)).astype(jnp.bfloat16)
+
+
+def dot_split(left, right):
+    (a, b), (c, d) = split(left), split(right)
+    return sum(jnp.dot(u, v, preferred_element_type=jnp.float32) for u, v in ((b, c), (a, d), (a, c)))
+
+
 def z_offset(turn):
     back = NZ - 1 - turn
     odd = back % 2
@@ -53,10 +63,11 @@
 
 def kernel(
     source_ref,
-    grad_ref,
+    grad_hbm,
     mom_hbm,
     ret_hbm,
     new_hbm,
+    grad_ref,
     mom,
     send,
     recv,
@@ -83,6 +94,8 @@
     my_e, _, _ = place(my_z, my_x, my_k)
 
     mom_in = pltpu.make_async_copy(mom_hbm, mom, local_sems.at[0])
+    grad_in = pltpu.make_async_copy(grad_hbm, grad_ref, local_sems.at[2])
+    grad_in.start()
     mom_in.start()
 
     barrier = pltpu.get_barrier_semaphore()
@@ -125,8 +138,7 @@
 
     gram[...] = jnp.zeros_like(gram)
 
-    def target_k(kk):
-        return ((my_y + kk // 2) % NY) * 2 + (my_core + kk % 2) % 2
+    target_k = [((my_y + kk // 2) % NY) * 2 + (my_core + kk % 2) % 2 for kk in range(ROW_SPLIT)]
 
     def remote(src, dst, one, two, to):
         return pltpu.make_async_remote_copy(
@@ -151,7 +163,7 @@
                 column = source_ref[group * BPG + h * HALF + j] * HD
                 stage[j] = grad_ref[:, pl.ds(column, HD)].astype(jnp.float32)
             for kk in range(ROW_SPLIT):
-                k = target_k(kk)
+                k = target_k[kk]
                 e, to_f, to_o = place(z, x, k)
                 parts = [stage[j, pl.ds(k, SUB, stride=ROW_SPLIT), :] for j in range(HALF)]
                 send[chunk_of(h * NDEV + e), :] = jnp.concatenate(parts, axis=0).astype(jnp.bfloat16)
@@ -240,42 +252,44 @@
             parts = []
             for j in range(HALF):
                 x = nest[h * HALF + j, pl.ds(pl.multiple_of(z * BATCH * SUB, BATCH * SUB), BATCH * SUB), :]
-                parts.append(dot(x, chain[h * HALF + j]).reshape(BATCH, SUB, HD))
+                parts.append(dot_split(x, chain[h * HALF + j]).reshape(BATCH, SUB, HD))
             rows = pl.ds(pl.multiple_of((h * NZ + z) * BATCH * CHUNK, BATCH * CHUNK), BATCH * CHUNK)
             back[rows, :] = jnp.stack(parts, axis=1).reshape(BATCH * CHUNK, HD).astype(jnp.bfloat16)
 
-            def give_turn(index, carry):
-                x = (my_x + index % NX) % NX
-                e, to_f, to_o = place(z, x, target_k(index // NX))
-                src, dst = back.at[chunk_of(h * NDEV + e), :], ret_hbm.at[chunk_of(h * NDEV + my_e), :]
-                give(src, dst, back_sems.at[0], back_sems.at[1], e, (to_f, to_o))
+            def give_row(r, carry):
+                x = (my_x + r) % NX
+                for kk in range(ROW_SPLIT):
+                    e, to_f, to_o = place(z, x, target_k[kk])
+                    src, dst = back.at[chunk_of(h * NDEV + e), :], ret_hbm.at[chunk_of(h * NDEV + my_e), :]
+                    if kk:
+                        remote(src, dst, back_sems.at[0], back_sems.at[1], (to_f, to_o)).start()
+                    else:
+                        give(src, dst, back_sems.at[0], back_sems.at[1], e, (to_f, to_o))
                 return carry
 
-            lax.fori_loop(0, BATCH, give_turn, 0)
+            lax.fori_loop(0, NX, give_row, 0)
             return carry
 
         lax.fori_loop(first, last, finish, 0)
 
+    grad_in.wait()
     send_turns(0, 0, NZ)
+    send_turns(1, 0, 4)
     mom_in.wait()
-    absorb_turns(0, 0, 6)
-    send_turns(1, 0, 2)
-    absorb_turns(0, 6, NZ)
+    absorb_turns(0, 0, NZ)
     pair_copy(0).start()
-    send_turns(1, 2, 3)
+    send_turns(1, 4, 5)
     ring_start(0)
-    send_turns(1, 3, NZ)
+    send_turns(1, 5, NZ)
     factors(0)
-    absorb_turns(1, 0, 6)
     chain_copy(0).wait()
-    finish_turns(0, 0, 2)
-    absorb_turns(1, 6, NZ)
+    finish_turns(0, 0, 4)
+    absorb_turns(1, 0, NZ)
     pair_copy(1).start()
-    finish_turns(0, 2, 3)
+    finish_turns(0, 4, 5)
     ring_start(1)
-    finish_turns(0, 3, 6)
+    finish_turns(0, 5, 8)
     factors(1)
-    finish_turns(0, 6, NZ)
     chain_copy(1).wait()
     finish_turns(1, 0, NZ)
 
@@ -305,10 +319,6 @@
             return carry
 
         lax.fori_loop(0, ROWS // PIECES // 128, widen, 0, unroll=2)
-
-    pltpu.make_async_copy(new_hbm, kept, out_sems.at[0]).wait()
-    for rows in rows_of:
-        pltpu.make_async_copy(kept.at[rows, :], kept_hbm.at[rows, :], out_sems.at[1]).start()
 
     columns = order_ref.shape[0] // PIECES
     for i in range(PIECES):
@@ -323,9 +333,13 @@
             out[:, pl.ds(pl.multiple_of(p * HD, HD), HD)] = jnp.concatenate(tiles, axis=0).astype(jnp.bfloat16)
             return carry
 
-        lax.fori_loop(0, columns, column, 0, unroll=4)
+        lax.fori_loop(0, columns, column, 0, unroll=8)
         panel = pl.ds(i * columns * HD, columns * HD)
         pltpu.make_async_copy(out.at[:, panel], out_hbm.at[:, panel], out_sems.at[2]).start()
+        if i == 0:
+            pltpu.make_async_copy(new_hbm, kept, out_sems.at[0]).wait()
+            for rows in rows_of:
+                pltpu.make_async_copy(kept.at[rows, :], kept_hbm.at[rows, :], out_sems.at[1]).start()
 
     pltpu.make_async_copy(kept, kept_hbm, out_sems.at[1]).wait()
     pltpu.make_async_copy(out, out_hbm, out_sems.at[2]).wait()
@@ -337,16 +351,17 @@
     source_of = jnp.sum(
         jnp.where(head_order[:, None] == positions[None, :], positions[:, None], 0), axis=0
     )
-    vmem, smem, hbm = (pl.BlockSpec(memory_space=m) for m in (pltpu.VMEM, pltpu.SMEM, pl.ANY))
+    smem, hbm = (pl.BlockSpec(memory_space=m) for m in (pltpu.SMEM, pl.ANY))
     returned, new = pl.pallas_call(
         kernel,
         out_shape=(
             jax.ShapeDtypeStruct((ROWS, HD), jnp.bfloat16),
             jax.ShapeDtypeStruct((ROWS, HD), jnp.float32),
         ),
-        in_specs=[smem, vmem, hbm],
+        in_specs=[smem, hbm, hbm],
         out_specs=(hbm, hbm),
         scratch_shapes=[
+            pltpu.VMEM(gradient.shape, jnp.bfloat16),
             pltpu.VMEM((ROWS, HD), jnp.float32),
             pltpu.VMEM((ROWS, HD), jnp.bfloat16),
             pltpu.VMEM((ROWS, HD), jnp.bfloat16),
@@ -363,7 +378,7 @@
             pltpu.SemaphoreType.DMA((2, 2)),
             pltpu.SemaphoreType.DMA((2, 2)),
             pltpu.SemaphoreType.DMA((2, 2)),
-            pltpu.SemaphoreType.DMA((2,)),
+            pltpu.SemaphoreType.DMA((3,)),
         ],
         compiler_params=pltpu.CompilerParams(
             collective_id=0, has_side_effects=True, vmem_limit_bytes=56 * 2**20

time: 138 us -> 131 us (0.949)
  Pallas kernels: 135 us -> 129 us
    pallas_call x1, Pallas kernels: 127 us -> 121 us  [per_device(): pl.pallas_call(kernel, out_shape=(jax.ShapeDtypeStruct((ROWS, HD), jnp.bf...]
where the time goes in v5:
time: 131 us
  Pallas kernels  129 us (98%)
    pallas_call x1, Pallas kernels, per_device(): pl.pallas_call(kernel, out_shape=(jax.ShapeDtypeStruct((ROWS, HD), jnp.bf...  121 us
    pallas_call x1, Pallas kernels, per_device(): pl.pallas_call(place_kernel, out_shape=(jax.ShapeDtypeStruct(gradient.sha...  8.28 us

profile of v5, /device:TPU:1, one launch (start us, length us, event | category | flops | bytes accessed | tf_op | source)
XLA Modules:
  0.0 130.9 jit_solution(3470890427653500605)
XLA Ops:
  0.6 1.3 select_reduce_fusion.source_ref
  1.9 120.7 %shard_map.50 = (bf16[8192,128]{1,0:T(8,128)(2,1)}, f32[8192,128]{1,0:T(8,128)}) custom-call(s32[128]{0:T(128)} %select_reduce_fusion.source_ref, bf16[64,16384]{1,0:T(8,128)(2,1)} %grad_hbm.1, f32[8192,128]{1,0:T(8,128)} %bitcast.2), custom_call_target="tpu_custom_call" | custom-call | tf_op jit(solution)/shard_map/pallas_call | solution.py:355
  122.6 8.3 %shard_map.51 = (bf16[64,16384]{1,0:T(8,128)(2,1)}, f32[8192,128]{1,0:T(8,128)}) custom-call(s32[128]{0:T(128)} %order_ref.1, bf16[8192,128]{1,0:T(8,128)(2,1)} %get-tuple-element.6.ret_hbm, f32[8192,128]{1,0:T(8,128)} %get-tuple-element.7.new_hbm), custom_call_target="tpu_custom_call" | custom-call | tf_op jit(solution)/shard_map/pallas_call | solution.py:387

commit v6 on v5

--- a/solution.py
+++ b/solution.py
@@ -62,11 +62,13 @@
 
 
 def kernel(
-    source_ref,
+    order_ref,
     grad_hbm,
     mom_hbm,
     ret_hbm,
     new_hbm,
+    source_row,
+    source_ref,
     grad_ref,
     mom,
     send,
@@ -98,6 +100,12 @@
     grad_in.start()
     mom_in.start()
 
+    down, along = (lax.broadcasted_iota(jnp.int32, (HD, HD), d) for d in range(2))
+    held = jnp.broadcast_to(order_ref[...], (HD, HD)).T
+    source_row[...] = jnp.max(jnp.where(held == along, down, 0), axis=0, keepdims=True)
+    source_in = pltpu.make_async_copy(source_row, source_ref, local_sems.at[3])
+    source_in.start()
+
     barrier = pltpu.get_barrier_semaphore()
 
     leader = (my_k == 0) & (o == 0)
@@ -160,7 +168,7 @@
             z, x = (my_z + z_offset(turn)) % NZ, (my_x + r) % NX
             group = (x // 2) * 16 + (x % 2) * NZ + z
             for j in range(HALF):
-                column = source_ref[group * BPG + h * HALF + j] * HD
+                column = source_ref[0, group * BPG + h * HALF + j] * HD
                 stage[j] = grad_ref[:, pl.ds(column, HD)].astype(jnp.float32)
             for kk in range(ROW_SPLIT):
                 k = target_k[kk]
@@ -273,6 +281,7 @@
         lax.fori_loop(first, last, finish, 0)
 
     grad_in.wait()
+    source_in.wait()
     send_turns(0, 0, NZ)
     send_turns(1, 0, 4)
     mom_in.wait()
@@ -303,22 +312,15 @@
 PIECES = 8
 
 
-def place_kernel(order_ref, ret_hbm, new_hbm, out_hbm, kept_hbm, ret, wide, out, kept, in_sems, out_sems):
-    rows_of = [pl.ds(i * (ROWS // PIECES), ROWS // PIECES) for i in range(PIECES)]
-    for i, rows in enumerate(rows_of):
-        pltpu.make_async_copy(ret_hbm.at[rows, :], ret.at[rows, :], in_sems.at[i]).start()
-    for rows in rows_of:
-        pltpu.make_async_copy(new_hbm.at[rows, :], kept.at[rows, :], out_sems.at[0]).start()
-
-    for i, rows in enumerate(rows_of):
-        pltpu.make_async_copy(ret_hbm.at[rows, :], ret.at[rows, :], in_sems.at[i]).wait()
-
-        def widen(index, carry):
-            some = pl.ds(pl.multiple_of(i * (ROWS // PIECES) + index * 128, 128), 128)
-            wide[some, :] = ret[some, :].astype(jnp.float32)
-            return carry
-
-        lax.fori_loop(0, ROWS // PIECES // 128, widen, 0, unroll=2)
+def place_kernel(order_ref, ret, new_ref, out_hbm, kept_hbm, wide, out, out_sems):
+    pltpu.make_async_copy(new_ref, kept_hbm, out_sems.at[0]).start()
+
+    def widen(index, carry):
+        rows = pl.ds(pl.multiple_of(index * 128, 128), 128)
+        wide[rows, :] = ret[rows, :].astype(jnp.float32)
+        return carry
+
+    lax.fori_loop(0, ROWS // 128, widen, 0, unroll=2)
 
     columns = order_ref.shape[0] // PIECES
     for i in range(PIECES):
@@ -335,32 +337,25 @@
 
         lax.fori_loop(0, columns, column, 0, unroll=8)
         panel = pl.ds(i * columns * HD, columns * HD)
-        pltpu.make_async_copy(out.at[:, panel], out_hbm.at[:, panel], out_sems.at[2]).start()
-        if i == 0:
-            pltpu.make_async_copy(new_hbm, kept, out_sems.at[0]).wait()
-            for rows in rows_of:
-                pltpu.make_async_copy(kept.at[rows, :], kept_hbm.at[rows, :], out_sems.at[1]).start()
-
-    pltpu.make_async_copy(kept, kept_hbm, out_sems.at[1]).wait()
-    pltpu.make_async_copy(out, out_hbm, out_sems.at[2]).wait()
+        pltpu.make_async_copy(out.at[:, panel], out_hbm.at[:, panel], out_sems.at[1]).start()
+
+    pltpu.make_async_copy(new_ref, kept_hbm, out_sems.at[0]).wait()
+    pltpu.make_async_copy(out, out_hbm, out_sems.at[1]).wait()
 
 
 def per_device(gradient, momentum, head_order):
-    blocks = head_order.shape[0]
-    positions = jnp.arange(blocks, dtype=jnp.int32)
-    source_of = jnp.sum(
-        jnp.where(head_order[:, None] == positions[None, :], positions[:, None], 0), axis=0
-    )
-    smem, hbm = (pl.BlockSpec(memory_space=m) for m in (pltpu.SMEM, pl.ANY))
+    vmem, smem, hbm = (pl.BlockSpec(memory_space=m) for m in (pltpu.VMEM, pltpu.SMEM, pl.ANY))
     returned, new = pl.pallas_call(
         kernel,
         out_shape=(
             jax.ShapeDtypeStruct((ROWS, HD), jnp.bfloat16),
             jax.ShapeDtypeStruct((ROWS, HD), jnp.float32),
         ),
-        in_specs=[smem, hbm, hbm],
+        in_specs=[vmem, hbm, hbm],
         out_specs=(hbm, hbm),
         scratch_shapes=[
+            pltpu.VMEM((1, HD), jnp.int32),
+            pltpu.SMEM((1, HD), jnp.int32),
             pltpu.VMEM(gradient.shape, jnp.bfloat16),
             pltpu.VMEM((ROWS, HD), jnp.float32),
             pltpu.VMEM((ROWS, HD), jnp.bfloat16),
@@ -378,29 +373,26 @@
             pltpu.SemaphoreType.DMA((2, 2)),
             pltpu.SemaphoreType.DMA((2, 2)),
             pltpu.SemaphoreType.DMA((2, 2)),
-            pltpu.SemaphoreType.DMA((3,)),
+            pltpu.SemaphoreType.DMA((4,)),
         ],
         compiler_params=pltpu.CompilerParams(
-            collective_id=0, has_side_effects=True, vmem_limit_bytes=56 * 2**20
+            collective_id=0, has_side_effects=True, vmem_limit_bytes=45 * 2**20
         ),
-    )(source_of, gradient, momentum.reshape(ROWS, HD))
+    )(head_order[None, :], gradient, momentum.reshape(ROWS, HD))
     placed, kept = pl.pallas_call(
         place_kernel,
         out_shape=(
             jax.ShapeDtypeStruct(gradient.shape, jnp.bfloat16),
             jax.ShapeDtypeStruct((ROWS, HD), jnp.float32),
         ),
-        in_specs=[smem, hbm, hbm],
+        in_specs=[smem, vmem, hbm],
         out_specs=(hbm, hbm),
         scratch_shapes=[
-            pltpu.VMEM((ROWS, HD), jnp.bfloat16),
             pltpu.VMEM((ROWS, HD), jnp.float32),
             pltpu.VMEM(gradient.shape, jnp.bfloat16),
-            pltpu.VMEM((ROWS, HD), jnp.float32),
-            pltpu.SemaphoreType.DMA((PIECES,)),
-            pltpu.SemaphoreType.DMA((3,)),
+            pltpu.SemaphoreType.DMA((2,)),
         ],
-        compiler_params=pltpu.CompilerParams(vmem_limit_bytes=58 * 2**20),
+        compiler_params=pltpu.CompilerParams(vmem_limit_bytes=16 * 2**20),
     )(head_order, returned, new)
     return (placed, kept.reshape(momentum.shape))
 

time: 131 us -> 129 us (0.985)
  Pallas kernels: 129 us -> 126 us
  local copies, waits for them, and re-layouts: 0 us -> 2.24 us
    pallas_call x1, Pallas kernels: 8.28 us -> 5.83 us  [per_device(): pl.pallas_call(place_kernel, out_shape=(jax.ShapeDtypeStruct(gradient.sha...]
    unnamed x0 -> x4, local copies, waits for them, and re-layouts: none -> 2.24 us
where the time goes in v6:
time: 129 us
  Pallas kernels  126 us (98%)
  local copies, waits for them, and re-layouts  2.24 us (2%)
    pallas_call x1, Pallas kernels, per_device(): pl.pallas_call(kernel, out_shape=(jax.ShapeDtypeStruct((ROWS, HD), jnp.bf...  120 us
    pallas_call x1, Pallas kernels, per_device(): pl.pallas_call(place_kernel, out_shape=(jax.ShapeDtypeStruct(gradient.sha...  5.83 us

profile of v6, /device:TPU:1, one launch (start us, length us, event | category | flops | bytes accessed | tf_op | source)
XLA Modules:
  0.0 128.8 jit_solution(4326190431316379782)
XLA Ops:
  0.6 0.0 copy-start
  0.6 1.6 %copy-done = bf16[64,16384]{1,0:T(8,128)(2,1)S(1)} copy-done((bf16[64,16384]{1,0:T(8,128)(2,1)S(1)}, bf16[64,16384]{1,0:T(8,128)(2,1)}, u32[]{:S(2)}) %copy-start) | copy-done | bytes 2097176
  2.2 0.0 copy-start.1
  2.2 0.7 copy-done.1
  2.9 120.0 %shard_map.50 = (bf16[8192,128]{1,0:T(8,128)(2,1)S(1)}, f32[8192,128]{1,0:T(8,128)S(1)}) custom-call(s32[1,128]{1,0:T(1,128)S(1)} %bitcast.3, bf16[64,16384]{1,0:T(8,128)(2,1)S(1)} %copy-done, f32[8192,128]{1,0:T(8,128)} %bitcast.4), custom_call_target="tpu_custom_call" | custom-call | tf_op jit(solution)/shard_map/pallas_call | solution.py:348
  122.9 5.8 %shard_map.51 = (bf16[64,16384]{1,0:T(8,128)(2,1)}, f32[8192,128]{1,0:T(8,128)}) custom-call(s32[128]{0:T(128)S(1)} %copy-done.1, bf16[8192,128]{1,0:T(8,128)(2,1)S(1)} %get-tuple-element.6.ret, f32[8192,128]{1,0:T(8,128)S(1)} %get-tuple-element.7.new_ref), custom_call_target="tpu_custom_call" | custom-call | tf_op jit(solution)/shard_map/pallas_call | solution.py:382
Async XLA Ops:
  0.6 1.6 %copy-start = (bf16[64,16384]{1,0:T(8,128)(2,1)S(1)}, bf16[64,16384]{1,0:T(8,128)(2,1)}, u32[]{:S(2)}) copy-start(bf16[64,16384]{1,0:T(8,128)(2,1)} %grad_hbm.1) | copy-start | bytes 6291460
  2.2 0.7 copy-start.1

commit v7 on v6

--- a/solution.py
+++ b/solution.py
@@ -63,13 +63,12 @@
 
 def kernel(
     order_ref,
-    grad_hbm,
+    grad_ref,
     mom_hbm,
     ret_hbm,
     new_hbm,
     source_row,
     source_ref,
-    grad_ref,
     mom,
     send,
     recv,
@@ -96,8 +95,6 @@
     my_e, _, _ = place(my_z, my_x, my_k)
 
     mom_in = pltpu.make_async_copy(mom_hbm, mom, local_sems.at[0])
-    grad_in = pltpu.make_async_copy(grad_hbm, grad_ref, local_sems.at[2])
-    grad_in.start()
     mom_in.start()
 
     down, along = (lax.broadcasted_iota(jnp.int32, (HD, HD), d) for d in range(2))
@@ -280,7 +277,6 @@
 
         lax.fori_loop(first, last, finish, 0)
 
-    grad_in.wait()
     source_in.wait()
     send_turns(0, 0, NZ)
     send_turns(1, 0, 4)
@@ -292,12 +288,12 @@
     send_turns(1, 5, NZ)
     factors(0)
     chain_copy(0).wait()
-    finish_turns(0, 0, 4)
+    finish_turns(0, 0, 3)
     absorb_turns(1, 0, NZ)
     pair_copy(1).start()
-    finish_turns(0, 4, 5)
+    finish_turns(0, 3, 4)
     ring_start(1)
-    finish_turns(0, 5, 8)
+    finish_turns(0, 4, NZ)
     factors(1)
     chain_copy(1).wait()
     finish_turns(1, 0, NZ)
@@ -351,12 +347,11 @@
             jax.ShapeDtypeStruct((ROWS, HD), jnp.bfloat16),
             jax.ShapeDtypeStruct((ROWS, HD), jnp.float32),
         ),
-        in_specs=[vmem, hbm, hbm],
+        in_specs=[vmem, vmem, hbm],
         out_specs=(hbm, hbm),
         scratch_shapes=[
             pltpu.VMEM((1, HD), jnp.int32),
             pltpu.SMEM((1, HD), jnp.int32),
-            pltpu.VMEM(gradient.shape, jnp.bfloat16),
             pltpu.VMEM((ROWS, HD), jnp.float32),
             pltpu.VMEM((ROWS, HD), jnp.bfloat16),
             pltpu.VMEM((ROWS, HD), jnp.bfloat16),

time: 129 us -> 128 us (level)
  Pallas kernels: 126 us -> 124 us
    pallas_call x1, Pallas kernels: 120 us -> 119 us  [per_device(): pl.pallas_call(kernel, out_shape=(jax.ShapeDtypeStruct((ROWS, HD), jnp.bf...]
where the time goes in v7:
time: 128 us; the launch traced here: 127 us
  Pallas kernels  124 us (97%)
  local copies, waits for them, and re-layouts  2.24 us (2%)
    pallas_call x1, Pallas kernels, per_device(): pl.pallas_call(kernel, out_shape=(jax.ShapeDtypeStruct((ROWS, HD), jnp.bf...  119 us
    pallas_call x1, Pallas kernels, per_device(): pl.pallas_call(place_kernel, out_shape=(jax.ShapeDtypeStruct(gradient.sha...  5.83 us

profile of v7, /device:TPU:1, one launch (start us, length us, event | category | flops | bytes accessed | tf_op | source)
XLA Modules:
  0.0 127.4 jit_solution(15166982615782795584)
XLA Ops:
  0.6 0.0 copy-start
  0.6 1.6 %copy-done = bf16[64,16384]{1,0:T(8,128)(2,1)S(1)} copy-done((bf16[64,16384]{1,0:T(8,128)(2,1)S(1)}, bf16[64,16384]{1,0:T(8,128)(2,1)}, u32[]{:S(2)}) %copy-start) | copy-done | bytes 2097176
  2.2 0.0 copy-start.1
  2.2 0.7 copy-done.1
  2.9 118.7 %shard_map.50 = (bf16[8192,128]{1,0:T(8,128)(2,1)S(1)}, f32[8192,128]{1,0:T(8,128)S(1)}) custom-call(s32[1,128]{1,0:T(1,128)S(1)} %bitcast.3, bf16[64,16384]{1,0:T(8,128)(2,1)S(1)} %copy-done, f32[8192,128]{1,0:T(8,128)} %bitcast.4), custom_call_target="tpu_custom_call" | custom-call | tf_op jit(solution)/shard_map/pallas_call | solution.py:344
  121.6 5.8 %shard_map.51 = (bf16[64,16384]{1,0:T(8,128)(2,1)}, f32[8192,128]{1,0:T(8,128)}) custom-call(s32[128]{0:T(128)S(1)} %copy-done.1, bf16[8192,128]{1,0:T(8,128)(2,1)S(1)} %get-tuple-element.6.ret, f32[8192,128]{1,0:T(8,128)S(1)} %get-tuple-element.7.new_ref), custom_call_target="tpu_custom_call" | custom-call | tf_op jit(solution)/shard_map/pallas_call | solution.py:377
Async XLA Ops:
  0.6 1.6 %copy-start = (bf16[64,16384]{1,0:T(8,128)(2,1)S(1)}, bf16[64,16384]{1,0:T(8,128)(2,1)}, u32[]{:S(2)}) copy-start(bf16[64,16384]{1,0:T(8,128)(2,1)} %grad_ref.1) | copy-start | bytes 6291460
  2.2 0.7 copy-start.1
